TPU v7x, 32 devices: a whole 2x2x4 slice. The times are simulated.
32 devices in a mesh: dp: 8 (over z, y), sub: 4 (over x, core).
Axes of the slice: x: 2, y: 2, z: 4, core: 2. Of those that a mesh axis runs over, the one named last changes fastest.
Arguments:
- activations: bfloat16 [65536, 768], P(('dp', 'sub')), may hold values from -20 to 20
- out_grad: bfloat16 [65536, 768], P(('dp', 'sub')), may hold values from -6 to 6
- species: int32 [65536], P(('dp', 'sub')), may hold values from 0 to 1, as said below
- first_start: int32 [32], P(('dp', 'sub')), may hold values from 0 to 1023, as said below
- species_weight: float32 [2, 768], replicated, may hold values from 0.5 to 2
- conv_weight: bfloat16 [3, 768, 384], P(None, 'dp', 'sub'), may hold values from -0.125 to 0.125
- point_weight: bfloat16 [384, 768], P('sub', 'dp'), may hold values from -0.3125 to 0.3125
- gain_one: float32 [768], replicated, may hold values from 0.1 to 1.9
- bias_one: float32 [768], replicated, may hold values from -3 to 3
- gain_two: float32 [384], replicated, may hold values from 0.1 to 1.9
- bias_two: float32 [384], replicated, may hold values from -3 to 3
- running_one: float32 [2, 768], replicated, may hold values from 0.5 to 2
- running_two: float32 [2, 384], replicated, may hold values from 0.5 to 2
Outputs:
- output: bfloat16 [65536, 768], P(('dp', 'sub'))
- input_grad: bfloat16 [65536, 768], P(('dp', 'sub'))
- conv_grad: float32 [3, 768, 384], P(None, 'dp', 'sub')
- point_grad: float32 [384, 768], P('sub', 'dp')
- gain_one_grad: float32 [768], replicated
- bias_one_grad: float32 [768], replicated
- gain_two_grad: float32 [384], replicated
- bias_two_grad: float32 [384], replicated
- running_one_new: float32 [2, 768], replicated
- running_two_new: float32 [2, 384], replicated
Inputs may be any that keep to these rules, and one draw needn't show every extreme that they name: `first_start`: sequence starts in a block follow every 1024 rows after the first; the first block begins with a sequence start and the last block's first start is at 1023. All rows of one sequence have the same species.
All inputs are finite; a program needn't handle non-finite values.
Results may differ from a plain program's by a relative error of at most 0.0053.
Values may be sent and summed in bfloat16 or wider, within the bound.
A program may use at most 128 MiB of HBM per device.

v0:
```python
import jax
import jax.numpy as jnp
from jax import lax
from jax.sharding import PartitionSpec as P

DILATION_BINS = 11
SEQ_LEN = 1024


EPSILON = 0.001
MOMENTUM = 0.9


def padded(block, sides, width):
    for axis, dim in sides:
        count = lax.axis_size(axis)
        forward = [(i, i + 1) for i in range(count - 1)]
        backward = [(target, source) for source, target in forward]
        low = lax.ppermute(
            lax.slice_in_dim(block, block.shape[dim] - width, None, axis=dim), axis, forward
        )
        high = lax.ppermute(lax.slice_in_dim(block, 0, width, axis=dim), axis, backward)
        block = jnp.concatenate([low, block, high], axis=dim)
    return block


def gelu_parts(value):
    logistic = jax.nn.sigmoid(1.702 * value)
    return (value * logistic, logistic + 1.702 * value * logistic * (1.0 - logistic))


def body(
    activations,
    out_grad,
    species,
    first_start,
    species_weight,
    conv_weight,
    point_weight,
    gain_one,
    bias_one,
    gain_two,
    bias_two,
    running_one,
    running_two,
):
    count_rows = activations.shape[0]
    total_rows = count_rows * lax.axis_size("dp") * lax.axis_size("sub")
    conv_full, point_full = (
        lax.all_gather(conv_weight, "dp", axis=1, tiled=True),
        lax.all_gather(point_weight, "dp", axis=1, tiled=True),
    )
    conv_full, point_full = (
        lax.all_gather(conv_full, "sub", axis=2, tiled=True),
        lax.all_gather(point_full, "sub", axis=0, tiled=True),
    )
    kernel, channels, hidden = conv_full.shape
    x_float = activations.astype(jnp.float32)
    sum_one, square_one = lax.psum(
        (jnp.sum(x_float, axis=0), jnp.sum(x_float * x_float, axis=0)), ("dp", "sub")
    )
    mean_one = sum_one / total_rows
    var_one = square_one / total_rows - mean_one * mean_one
    inv_one = lax.rsqrt(var_one + EPSILON)
    x_hat = (x_float - mean_one) * inv_one
    pre_one = gain_one * x_hat + bias_one
    act_one, slope_one = gelu_parts(pre_one)
    activation_narrow = act_one.astype(jnp.bfloat16)
    row_position = jnp.arange(count_rows, dtype=jnp.int32)
    offset = first_start[0]
    sequence_count = count_rows // SEQ_LEN
    segment_label = jnp.where(row_position >= offset, (row_position - offset) // SEQ_LEN + 1, 0)
    leading_flag = (segment_label == 0).astype(jnp.bfloat16)
    trailing_flag = (segment_label == sequence_count).astype(jnp.bfloat16)
    broad_activation, broad_leading, broad_trailing = (
        padded(activation_narrow, ((("dp", "sub"), 0),), DILATION_BINS),
        padded(leading_flag, ((("dp", "sub"), 0),), DILATION_BINS),
        padded(trailing_flag, ((("dp", "sub"), 0),), DILATION_BINS),
    )
    previous_label = jnp.concatenate(
        [jnp.zeros((DILATION_BINS,), jnp.int32), segment_label[: count_rows - DILATION_BINS]]
    )
    next_label = jnp.concatenate(
        [segment_label[DILATION_BINS:], jnp.zeros((DILATION_BINS,), jnp.int32)]
    )
    before = jnp.where(
        row_position >= DILATION_BINS,
        previous_label == segment_label,
        (broad_trailing[:count_rows] > 0) & (segment_label == 0),
    )
    following_rows = jnp.where(
        row_position < count_rows - DILATION_BINS,
        next_label == segment_label,
        (broad_leading[2 * DILATION_BINS :] > 0) & (segment_label == sequence_count),
    )
    previous_mask = before.astype(jnp.bfloat16)[:, None]
    next_mask = following_rows.astype(jnp.bfloat16)[:, None]
    stacked_rows = jnp.concatenate(
        [
            previous_mask * broad_activation[:count_rows],
            activation_narrow,
            next_mask * broad_activation[2 * DILATION_BINS :],
        ],
        axis=1,
    )
    conv_out = jnp.dot(
        stacked_rows,
        conv_full.reshape(kernel * channels, hidden),
        preferred_element_type=jnp.float32,
    )
    sum_two, square_two = lax.psum(
        (jnp.sum(conv_out, axis=0), jnp.sum(conv_out * conv_out, axis=0)), ("dp", "sub")
    )
    mean_two = sum_two / total_rows
    var_two = square_two / total_rows - mean_two * mean_two
    inv_two = lax.rsqrt(var_two + EPSILON)
    z_hat = (conv_out - mean_two) * inv_two
    pre_two = gain_two * z_hat + bias_two
    act_two, slope_two = gelu_parts(pre_two)
    act_two_low = act_two.astype(jnp.bfloat16)
    branch = jnp.dot(act_two_low, point_full, preferred_element_type=jnp.float32)
    output = (x_float + branch).astype(jnp.bfloat16)
    row_weight = jnp.where(species[:, None] == 0, species_weight[0], species_weight[1])
    out_cot = out_grad.astype(jnp.float32) * row_weight
    grad_low = out_cot.astype(jnp.bfloat16)
    point_grad = lax.dot_general(
        act_two_low, grad_low, (((0,), (0,)), ((), ())), preferred_element_type=jnp.float32
    )
    act_two_grad = lax.dot_general(
        grad_low, point_full, (((1,), (1,)), ((), ())), preferred_element_type=jnp.float32
    )
    pre_two_grad = act_two_grad * slope_two
    bias_two_grad, gain_two_grad = lax.psum(
        (jnp.sum(pre_two_grad, axis=0), jnp.sum(pre_two_grad * z_hat, axis=0)), ("dp", "sub")
    )
    conv_cot = (
        inv_two
        * gain_two
        * (pre_two_grad - bias_two_grad / total_rows - z_hat * gain_two_grad / total_rows)
    )
    cotangent_narrow = conv_cot.astype(jnp.bfloat16)
    conv_grad = lax.dot_general(
        stacked_rows, cotangent_narrow, (((0,), (0,)), ((), ())), preferred_element_type=jnp.float32
    ).reshape(kernel, channels, hidden)
    broad_cotangent = padded(cotangent_narrow, ((("dp", "sub"), 0),), DILATION_BINS)
    back_in = jnp.concatenate(
        [
            next_mask * broad_cotangent[2 * DILATION_BINS :],
            cotangent_narrow,
            previous_mask * broad_cotangent[:count_rows],
        ],
        axis=1,
    )
    conv_back = jnp.transpose(conv_full, (0, 2, 1)).reshape(kernel * hidden, channels)
    act_one_grad = jnp.dot(back_in, conv_back, preferred_element_type=jnp.float32)
    pre_one_grad = act_one_grad * slope_one
    bias_one_grad, gain_one_grad = lax.psum(
        (jnp.sum(pre_one_grad, axis=0), jnp.sum(pre_one_grad * x_hat, axis=0)), ("dp", "sub")
    )
    input_grad = out_cot + inv_one * gain_one * (
        pre_one_grad - bias_one_grad / total_rows - x_hat * gain_one_grad / total_rows
    )
    conv_grad, point_grad = (
        lax.psum_scatter(conv_grad, "dp", scatter_dimension=1, tiled=True),
        lax.psum_scatter(point_grad, "dp", scatter_dimension=1, tiled=True),
    )
    conv_grad, point_grad = (
        lax.psum_scatter(conv_grad, "sub", scatter_dimension=2, tiled=True),
        lax.psum_scatter(point_grad, "sub", scatter_dimension=0, tiled=True),
    )
    unbias = total_rows / (total_rows - 1.0)
    running_one_new = MOMENTUM * running_one + (1.0 - MOMENTUM) * jnp.stack(
        [mean_one, var_one * unbias]
    )
    running_two_new = MOMENTUM * running_two + (1.0 - MOMENTUM) * jnp.stack(
        [mean_two, var_two * unbias]
    )
    return (
        output,
        input_grad.astype(jnp.bfloat16),
        conv_grad,
        point_grad,
        gain_one_grad,
        bias_one_grad,
        gain_two_grad,
        bias_two_grad,
        running_one_new,
        running_two_new,
    )


def solution(mesh):
    in_specs = (
        P(("dp", "sub"), None),
        P(("dp", "sub"), None),
        P(("dp", "sub")),
        P(("dp", "sub")),
        P(),
        P(None, "dp", "sub"),
        P("sub", "dp"),
        P(),
        P(),
        P(),
        P(),
        P(),
        P(),
    )
    out_specs = (
        P(("dp", "sub"), None),
        P(("dp", "sub"), None),
        P(None, "dp", "sub"),
        P("sub", "dp"),
        P(),
        P(),
        P(),
        P(),
        P(),
        P(),
    )
    return jax.shard_map(body, mesh=mesh, in_specs=in_specs, out_specs=out_specs, check_vma=False)
```

profile of v0, /device:TPU:0, one launch (start us, length us, event | category | flops | bytes accessed | tf_op | source)
XLA Modules:
  0.0 467.3 jit_solution(10512179398251475126)
XLA Ops:
  7.3 1.1 copy.32
  8.3 36.0 %all_gather.12 = bf16[3,768,96]{2,0,1:T(4,128)(2,1)} all-gather(bf16[3,96,96]{2,0,1:T(4,128)(2,1)S(1)} %copy.32), channel_id=1, replica_groups=mesh['dp'=8,'sub'=4] {'dp'}, dimensions={1}, use_global_device_ids=true | all-gather | bytes 497664 | tf_op jit(solution)/shard_map/all_gather | solution.py:50
  44.4 2.1 copy.33
  46.6 2.8 fusion.14
  49.3 40.0 %all-reduce.5 = (f32[768]{0:T(1024)S(1)}, f32[768]{0:T(1024)S(1)}) all-reduce(f32[768]{0:T(1024)S(1)} %get-tuple-element.67, f32[768]{0:T(1024)S(1)} %get-tuple-element.66), channel_id=1, replica_groups=mesh['dp'=8,'sub'=4] {'dp','sub'}, use_global_device_ids=true, to_apply=%region_1.0 | all-reduce | flops 1536 | bytes 12288 | tf_op jit(solution)/shard_map/psum | solution.py:59
  89.3 0.6 broadcast_multiply_fusion
  89.9 2.4 fusion.7
  92.4 1.7 copy-done.1
  94.0 1.9 collective-permute-start.1
  95.9 1.3 collective-permute-start.3
  97.9 0.6 slice.71
  98.5 5.5 %collective-permute-start = (bf16[11]{0:T(256)(128)(2,1)}, bf16[11]{0:T(256)(128)(2,1)}, u32[]{:S(2)}, u32[]{:S(2)}) collective-permute-start(bf16[11]{0:T(256)(128)(2,1)} %slice.71), channel_id=1, source_target_pairs={{0,1},{1,2},{2,3},{3,4},{4,5},{5,6},{6,7},{7,8},{8,9},{9,10},{10,1... | collective-permute-start | bytes 74 | tf_op jit(solution)/shard_map/ppermute | solution.py:19
  104.5 1.3 collective-permute-start.2
  105.9 34.3 %all_gather.14 = bf16[96,768]{0,1:T(8,128)(2,1)S(1)} all-gather(bf16[96,96]{0,1:T(8,128)(2,1)S(1)} %copy.35), channel_id=1, replica_groups=mesh['dp'=8,'sub'=4] {'dp'}, dimensions={1}, use_global_device_ids=true | all-gather | bytes 165888 | tf_op jit(solution)/shard_map/all_gather | solution.py:51
  140.4 0.8 slice_reduce_fusion.1
  141.2 7.1 %all_gather.15 = bf16[384,768]{1,0:T(8,128)(2,1)} all-gather(bf16[96,768]{1,0:T(8,128)(2,1)S(1)} %copy.36), channel_id=1, replica_groups=mesh['dp'=8,'sub'=4] {'sub'}, dimensions={0}, use_global_device_ids=true | all-gather | bytes 737280 | tf_op jit(solution)/shard_map/all_gather | solution.py:55
  148.3 0.7 broadcast_compare_fusion.2
  149.1 0.8 fusion.40
  149.9 0.8 fusion.42
  150.6 7.0 %fusion.26 = (bf16[2048,768]{1,0:T(8,128)(2,1)}, bf16[2048,768]{1,0:T(8,128)(2,1)}) fusion(bf16[2048,768]{1,0:T(8,128)(2,1)} %copy-done.1, bf16[11,768]{1,0:T(8,128)(2,1)} %collective-permute-done.1, bf16[2048]{0:T(1024)(128)(2,1)S(1)} %fusion.40, bf16[11,768]{1,0:T(8,128)(2,1)} %collective-permute-done.3, bf16[2048]{0:T(1024)(128)(2,1)S(1)} %fusion.42), kind=kLoop, calls=%fused_computation.36 | loop fusion | flops 18874368 | bytes 9479168 | tf_op jit(solution)/shard_map/mul | solution.py:100
  157.7 3.9 copy.34
  161.5 9.4 %multiply_reduce_fusion.1 = (f32[384]{0:T(512)S(1)}, f32[384]{0:T(512)S(1)}, f32[2048,384]{1,0:T(8,128)}) fusion(bf16[2304,384]{1,0:T(8,128)(2,1)} %bitcast.22, bf16[2048,768]{1,0:T(8,128)(2,1)} %get-tuple-element.79, bf16[2048,768]{1,0:T(8,128)(2,1)} %copy-done.1, bf16[2048,768]{1,0:T(8,128)(2,1)} %get-tuple-element.78), kind=kOutput, calls=%fused_computation.43 | convolution fusion | flops 3654548480 | bytes 14355456 | tf_op jit(solution)/shard_map/dot_general | solution.py:106
  170.9 38.0 %all-reduce.4 = (f32[384]{0:T(512)S(1)}, f32[384]{0:T(512)S(1)}) all-reduce(f32[384]{0:T(512)S(1)} %get-tuple-element.65, f32[384]{0:T(512)S(1)} %get-tuple-element.64), channel_id=1, replica_groups=mesh['dp'=8,'sub'=4] {'dp','sub'}, use_global_device_ids=true, to_apply=%region_5.6 | all-reduce | flops 768 | bytes 6144 | tf_op jit(solution)/shard_map/psum | solution.py:111
  208.9 6.5 %fusion.53 = (f32[384]{0:T(512)S(1)}, f32[384]{0:T(512)S(1)}, f32[2048,384]{1,0:T(8,128)}) fusion(f32[384]{0:T(512)S(1)} %get-tuple-element.93, f32[2048,384]{1,0:T(8,128)} %get-tuple-element.96, f32[384]{0:T(512)S(1)} %get-tuple-element.95, f32[384]{0:T(512)S(1)} %copy-done.20, f32[384]{0:T(512)S(1)} %copy-done.18, bf16[384,768]{1,0:T(8,128)(2,1)} %all_gather.15, ...), kind=kOutput, calls=%fused_computation.99 | convolution fusion | flops 1226833152 | bytes 10044416 | tf_op jit(solution)/shard_map/dot_general | solution.py:129
  215.4 41.2 %all-reduce.3 = (f32[384]{0:T(512)S(1)}, f32[384]{0:T(512)S(1)}) all-reduce(f32[384]{0:T(512)S(1)} %get-tuple-element.63, f32[384]{0:T(512)S(1)} %get-tuple-element.62), channel_id=1, replica_groups=mesh['dp'=8,'sub'=4] {'dp','sub'}, use_global_device_ids=true, to_apply=%region_11.12 | all-reduce | flops 768 | bytes 6144 | tf_op jit(solution)/shard_map/psum | solution.py:133
  256.6 3.8 multiply_convert_fusion
  260.5 0.9 copy-done.5
  261.3 6.7 %fusion.23 = f32[2304,384]{1,0:T(8,128)} fusion(bf16[2048,384]{1,0:T(8,128)(2,1)S(1)} %multiply_convert_fusion, bf16[2048,768]{1,0:T(8,128)(2,1)} %get-tuple-element.79, bf16[2048,768]{1,0:T(8,128)(2,1)S(1)} %copy-done.2, bf16[2048,768]{1,0:T(8,128)(2,1)S(1)} %copy-done.5), kind=kOutput, calls=%fused_computation.31 | convolution fusion | flops 3652190208 | bytes 14548992 | tf_op jit(solution)/shard_map/dot_general | solution.py:142
  268.1 6.7 %fusion.31 = f32[384,768]{0,1:T(8,128)} fusion(bf16[2048,768]{1,0:T(8,128)(2,1)} %param.14, f32[768]{0:T(1024)S(1)} %get-tuple-element.69, f32[768]{0:T(1024)S(1)} %get-tuple-element.68, pred[2048]{0:T(1024)(128)(4,1)S(1)} %broadcast_compare_fusion.2, f32[2048,384]{1,0:T(8,128)} %get-tuple-element.96, f32[384]{0:T(512)S(1)} %copy-done.20, ...), kind=kOutput, calls=%fused_computation.49 | convolution fusion | flops 1222115328 | bytes 7485440 | tf_op jit(solution)/shard_map/dot_general | solution.py:126
  274.9 0.6 fusion.43
  275.5 0.7 fusion.55
  276.2 1.3 collective-permute-start.4
  277.5 3.0 collective-permute-start.5
  280.6 6.4 %fusion.15 = bf16[2048,768]{1,0:T(8,128)(2,1)} fusion(bf16[2048,768]{1,0:T(8,128)(2,1)S(1)} %copy-done, bf16[384,768]{1,0:T(8,128)(2,1)} %all_gather.15, f32[2048,384]{1,0:T(8,128)} %get-tuple-element.96, f32[384]{0:T(512)S(1)} %copy-done.20, f32[384]{0:T(512)S(1)} %get-tuple-element.93, f32[384]{0:T(512)S(1)} %get-tuple-element.95, f32[384]{0:T(512)S(1)} %copy-done.18), kind=kOutput, calls=%fused_computation.20 | convolution fusion | flops 1220542464 | bytes 10033152 | tf_op jit(solution)/shard_map/dot_general | solution.py:121
  287.0 0.6 fusion.46
  287.6 3.0 fusion.30
  290.5 57.1 %reduce-scatter.9.cloned.1.call-done = f32[3,96,384]{2,1,0:T(8,128)} async-done(((f32[3,768,384]{2,1,0:T(8,128)}), f32[3,96,384]{2,1,0:T(8,128)}) %reduce-scatter.9.cloned.1.call-update) | async-done | bytes 442384 | tf_op jit(solution)/shard_map/reduce_scatter | solution.py:164
  347.6 2.2 copy.38
  349.8 2.3 reshape.50
  352.4 10.7 %fusion.52 = (f32[768]{0:T(1024)S(1)}, f32[768]{0:T(1024)S(1)}, f32[2048,768]{1,0:T(8,128)}) fusion(f32[768]{0:T(1024)S(1)} %get-tuple-element.88, f32[768]{0:T(1024)S(1)} %get-tuple-element.94, bf16[2048,768]{1,0:T(8,128)(2,1)S(1)} %copy-done, f32[768]{0:T(1024)S(1)} %copy-done.13, f32[768]{0:T(1024)S(1)} %copy-done.7, bf16[1152,768]{1,0:T(8,128)(2,1)} %bitcast.21, ...), kind=kOutput, calls=%fused_computation.98 | convolution fusion | flops 3664771584 | bytes 15943680 | tf_op jit(solution)/shard_map/dot_general | solution.py:155
  363.1 40.3 %all-reduce.2 = (f32[768]{0:T(1024)S(1)}, f32[768]{0:T(1024)S(1)}) all-reduce(f32[768]{0:T(1024)S(1)} %get-tuple-element.61, f32[768]{0:T(1024)S(1)} %get-tuple-element.60), channel_id=1, replica_groups=mesh['dp'=8,'sub'=4] {'dp','sub'}, use_global_device_ids=true, to_apply=%region_15.16 | all-reduce | flops 1536 | bytes 12288 | tf_op jit(solution)/shard_map/psum | solution.py:157
  403.4 11.3 %reduce-scatter.11.cloned.1.call-done = f32[384,96]{0,1:T(8,128)} async-done(((f32[384,768]{0,1:T(8,128)}), f32[384,96]{0,1:T(8,128)}) %reduce-scatter.11.cloned.1.call-update) | async-done | bytes 147472 | tf_op jit(solution)/shard_map/reduce_scatter | solution.py:165
  414.7 1.7 copy.40
  416.5 6.2 %fusion.13 = bf16[2048,768]{1,0:T(8,128)(2,1)} fusion(bf16[2048,768]{1,0:T(8,128)(2,1)S(1)} %copy-done, f32[2048,768]{1,0:T(8,128)} %get-tuple-element.98, bf16[2048,768]{1,0:T(8,128)(2,1)} %param.14, f32[768]{0:T(1024)S(1)} %get-tuple-element.70, f32[768]{0:T(1024)S(1)} %broadcast_multiply_fusion.1, f32[768]{0:T(1024)S(1)} %get-tuple-element.87, ...), kind=kLoop, calls=%fused_computation.18 | loop fusion | flops 20447232 | bytes 15752192 | tf_op jit(solution)/shard_map/convert_element_type | solution.py:180
  422.7 15.4 %reduce-scatter.13.cloned.1.call-done = f32[96,288]{1,0:T(8,128)} async-done(((f32[384,288]{1,0:T(8,128)}), f32[96,288]{1,0:T(8,128)}) %reduce-scatter.13.cloned.1.call-update) | async-done | bytes 110608
  438.1 1.0 reshape.51
  439.2 0.8 copy.39
  440.0 20.8 %reduce-scatter.15.cloned.1.call-done = f32[96,96]{1,0:T(8,128)} async-done(((f32[384,96]{1,0:T(8,128)}), f32[96,96]{1,0:T(8,128)}) %reduce-scatter.15.cloned.1.call-update) | async-done | bytes 36880
  (72 shorter events, 1.5 us)
Async XLA Ops:
  7.2 82.7 %copy-start = (bf16[2048,768]{1,0:T(8,128)(2,1)S(1)}, bf16[2048,768]{1,0:T(8,128)(2,1)}, u32[]{:S(2)}) copy-start(bf16[2048,768]{1,0:T(8,128)(2,1)} %param.13) | copy-start | bytes 9437188
  7.2 82.1 %copy-start.7 = (f32[768]{0:T(1024)S(1)}, f32[768]{0:T(1024)}, u32[]{:S(2)}) copy-start(f32[768]{0:T(1024)} %param.20) | copy-start | bytes 9220
  7.2 82.7 %copy-start.12 = (f32[768]{0:T(1024)S(1)}, f32[768]{0:T(1024)}, u32[]{:S(2)}) copy-start(f32[768]{0:T(1024)} %param.21) | copy-start | bytes 9220
  7.2 150.4 %all-gather.2.cloned.1.call-start = ((), (), s32[]{:S(2)}) async-start(), calls=%async_computation.4 | async-start | bytes 2211840 | tf_op jit(solution)/shard_map/all_gather | solution.py:54
  46.5 301.1 %reduce-scatter.9.cloned.1.call-start = ((), (), s32[]{:S(2)}) async-start(), calls=%async_computation.5 | async-start | bytes 3981312 | tf_op jit(solution)/shard_map/reduce_scatter | solution.py:164
  89.9 15.9 %copy-start.6 = (bf16[96,96]{1,0:T(8,128)(2,1)S(1)}, bf16[96,96]{1,0:T(8,128)(2,1)}, u32[]{:S(2)}) copy-start(bf16[96,96]{1,0:T(8,128)(2,1)} %param.19) | copy-start | bytes 55300
  92.3 1.7 copy-start.1
  94.0 56.6 %collective-permute-start.1 = (bf16[11,768]{1,0:T(8,128)(2,1)S(1)}, bf16[11,768]{1,0:T(8,128)(2,1)}, u32[]{:S(2)}, u32[]{:S(2)}) collective-permute-start(bf16[11,768]{1,0:T(8,128)(2,1)S(1)} %get-tuple-element.80), channel_id=1, source_target_pairs={{0,1},{1,2},{2,3},{3,4},{4,5},{5,6},{6,7},{7,8},{8,9},{9,10},{10,1... | collective-permute-start | bytes 50696 | tf_op jit(solution)/shard_map/ppermute | solution.py:19
  95.9 54.7 %collective-permute-start.3 = (bf16[11,768]{1,0:T(8,128)(2,1)S(1)}, bf16[11,768]{1,0:T(8,128)(2,1)}, u32[]{:S(2)}, u32[]{:S(2)}) collective-permute-start(bf16[11,768]{1,0:T(8,128)(2,1)S(1)} %get-tuple-element.81), channel_id=1, source_target_pairs={{1,0},{2,1},{3,2},{4,3},{5,4},{6,5},{7,6},{8,7},{9,8},{10,9},{11,1... | collective-permute-start | bytes 50696 | tf_op jit(solution)/shard_map/ppermute | solution.py:22
  97.9 6.1 %copy-start.10 = (bf16[2048]{0:T(1024)(128)(2,1)}, bf16[2048]{0:T(1024)(128)(2,1)S(1)}, u32[]{:S(2)}) copy-start(bf16[2048]{0:T(1024)(128)(2,1)S(1)} %fusion.44) | copy-start | bytes 12292
  98.5 50.6 %collective-permute-start = (bf16[11]{0:T(256)(128)(2,1)}, bf16[11]{0:T(256)(128)(2,1)}, u32[]{:S(2)}, u32[]{:S(2)}) collective-permute-start(bf16[11]{0:T(256)(128)(2,1)} %slice.71), channel_id=1, source_target_pairs={{0,1},{1,2},{2,3},{3,4},{4,5},{5,6},{6,7},{7,8},{8,9},{9,10},{10,1... | collective-permute-start | bytes 74 | tf_op jit(solution)/shard_map/ppermute | solution.py:19
  104.0 1.9 copy-start.9
  104.5 45.3 %collective-permute-start.2 = (bf16[11]{0:T(256)(128)(2,1)}, bf16[11]{0:T(256)(128)(2,1)}, u32[]{:S(2)}, u32[]{:S(2)}) collective-permute-start(bf16[11]{0:T(256)(128)(2,1)} %slice.74), channel_id=1, source_target_pairs={{1,0},{2,1},{3,2},{4,3},{5,4},{6,5},{7,6},{8,7},{9,8},{10,9},{11,1... | collective-permute-start | bytes 74 | tf_op jit(solution)/shard_map/ppermute | solution.py:22
  161.5 47.4 %copy-start.18 = (f32[384]{0:T(512)S(1)}, f32[384]{0:T(512)}, u32[]{:S(2)}) copy-start(f32[384]{0:T(512)} %param.22) | copy-start | bytes 4612
  161.5 47.4 %copy-start.20 = (f32[384]{0:T(512)S(1)}, f32[384]{0:T(512)}, u32[]{:S(2)}) copy-start(f32[384]{0:T(512)} %param.23) | copy-start | bytes 4612
  256.6 3.8 copy-start.17
  256.6 3.8 copy-start.19
  256.6 3.8 copy-start.2
  256.6 4.7 %copy-start.5 = (bf16[2048,768]{1,0:T(8,128)(2,1)S(1)}, bf16[2048,768]{1,0:T(8,128)(2,1)}, u32[]{:S(2)}) copy-start(bf16[2048,768]{1,0:T(8,128)(2,1)} %get-tuple-element.78) | copy-start | bytes 9437188
  261.3 6.7 %copy-start.3 = (bf16[2048,384]{1,0:T(8,128)(2,1)}, bf16[2048,384]{1,0:T(8,128)(2,1)S(1)}, u32[]{:S(2)}) copy-start(bf16[2048,384]{1,0:T(8,128)(2,1)S(1)} %multiply_convert_fusion) | copy-start | bytes 4718596
  268.0 6.8 %copy-start.8 = (f32[768]{0:T(1024)S(1)}, f32[768]{0:T(1024)}, u32[]{:S(2)}) copy-start(f32[768]{0:T(1024)} %get-tuple-element.86) | copy-start | bytes 9220
  268.1 6.8 %copy-start.11 = (f32[2,768]{1,0:T(2,128)S(1)}, f32[2,768]{1,0:T(2,128)}, u32[]{:S(2)}) copy-start(f32[2,768]{1,0:T(2,128)} %param.24) | copy-start | bytes 18436
  268.1 146.6 %reduce-scatter.11.cloned.1.call-start = ((), (), s32[]{:S(2)}) async-start(), calls=%async_computation.6 | async-start | bytes 1327104 | tf_op jit(solution)/shard_map/reduce_scatter | solution.py:165
  274.8 163.3 %reduce-scatter.13.cloned.1.call-start = ((), (), s32[]{:S(2)}) async-start(), calls=%async_computation.7 | async-start | bytes 737280
  276.2 11.3 %collective-permute-start.4 = (bf16[11,384]{1,0:T(8,128)(2,1)S(1)}, bf16[11,384]{1,0:T(8,128)(2,1)S(1)}, u32[]{:S(2)}, u32[]{:S(2)}) collective-permute-start(bf16[11,384]{1,0:T(8,128)(2,1)S(1)} %get-tuple-element.84), channel_id=1, source_target_pairs={{1,0},{2,1},{3,2},{4,3},{5,4},{6,5},{7,6},{8,7},{9,8},{10,9},{11,1... | collective-permute-start | bytes 25352 | tf_op jit(solution)/shard_map/ppermute | solution.py:22
  277.5 10.0 %collective-permute-start.5 = (bf16[11,384]{1,0:T(8,128)(2,1)S(1)}, bf16[11,384]{1,0:T(8,128)(2,1)S(1)}, u32[]{:S(2)}, u32[]{:S(2)}) collective-permute-start(bf16[11,384]{1,0:T(8,128)(2,1)S(1)} %get-tuple-element.85), channel_id=1, source_target_pairs={{0,1},{1,2},{2,3},{3,4},{4,5},{5,6},{6,7},{7,8},{8,9},{9,10},{10,1... | collective-permute-start | bytes 25352 | tf_op jit(solution)/shard_map/ppermute | solution.py:19
  280.6 6.4 %copy-start.16 = (f32[2,384]{1,0:T(2,128)S(1)}, f32[2,384]{1,0:T(2,128)}, u32[]{:S(2)}) copy-start(f32[2,384]{1,0:T(2,128)} %param.25) | copy-start | bytes 9220
  280.6 7.0 %copy-start.4 = (bf16[2048,384]{1,0:T(8,128)(2,1)S(1)}, bf16[2048,384]{1,0:T(8,128)(2,1)}, u32[]{:S(2)}) copy-start(bf16[2048,384]{1,0:T(8,128)(2,1)} %copy-done.3) | copy-start | bytes 4718596
  287.5 64.8 %copy-start.13 = (f32[768]{0:T(1024)S(1)}, f32[768]{0:T(1024)}, u32[]{:S(2)}) copy-start(f32[768]{0:T(1024)} %param.21) | copy-start | bytes 9220
  352.1 108.6 %reduce-scatter.15.cloned.1.call-start = ((), (), s32[]{:S(2)}) async-start(), calls=%async_computation.8 | async-start | bytes 245760
  403.4 19.3 %copy-start.14 = (f32[768]{0:T(1024)}, f32[768]{0:T(1024)S(1)}, u32[]{:S(2)}) copy-start(f32[768]{0:T(1024)S(1)} %get-tuple-element.70) | copy-start | bytes 9220
  403.4 19.3 %copy-start.15 = (f32[768]{0:T(1024)}, f32[768]{0:T(1024)S(1)}, u32[]{:S(2)}) copy-start(f32[768]{0:T(1024)S(1)} %get-tuple-element.71) | copy-start | bytes 9220
Sparse Core Ops, SparseCore 0:
  46.6 21.9 all-gather.1
  268.2 79.3 reduce-scatter.8
  351.0 63.6 reduce-scatter.10
  417.1 20.9 reduce-scatter.12
  441.0 19.7 reduce-scatter.14
where the time goes:
time: 469 us; the launch traced here: 467 us
  blocking collectives  237 us (51%)
  waiting for transfers between devices  105 us (22%)
  matrix products  46.3 us (10%)
  other arithmetic  29.3 us (6%)
  local copies, waits for them, and re-layouts  20.7 us (4%)
  between operations  14.8 us (3%)
  starting transfers between devices  14.7 us (3%)
    reduce_scatter x1, waiting for transfers between devices, body(): lax.psum_scatter(conv_grad, 'dp', scatter_dimension=1, tiled=True)  57.1 us
    psum x1, blocking collectives, body(): lax.psum((jnp.sum(pre_two_grad, axis=0), jnp.sum(pre_two_grad * z_hat, ax...  41.2 us
    psum x1, blocking collectives, body(): lax.psum((jnp.sum(pre_one_grad, axis=0), jnp.sum(pre_one_grad * x_hat, ax...  40.3 us
    psum x1, blocking collectives, body(): lax.psum((jnp.sum(x_float, axis=0), jnp.sum(x_float * x_float, axis=0)),...  40 us
    psum x1, blocking collectives, body(): lax.psum((jnp.sum(conv_out, axis=0), jnp.sum(conv_out * conv_out, axis=0)...  38 us
    unnamed x7, waiting for transfers between devices  36.3 us
    all_gather x1, blocking collectives, body(): lax.all_gather(conv_weight, 'dp', axis=1, tiled=True)  36 us
    all_gather x1, blocking collectives, body(): lax.all_gather(point_weight, 'dp', axis=1, tiled=True)  34.3 us
  transfers between devices with their start and end apart: 11, of which 4 were waited for; matrix products, arithmetic and copies ran while one was open for 13% of the time, Pallas kernels for 0%

commit v1 on v0

v1 whole, which is shorter than its diff:
```python
import functools

import jax
import jax.numpy as jnp
from jax import lax
from jax.experimental import pallas as pl
from jax.experimental.pallas import tpu as pltpu
from jax.sharding import PartitionSpec as P

DIL = 11
SEQ_LEN = 1024
EPSILON = 0.001
MOMENTUM = 0.9
PAD = 16
HALF_SLOPE = 0.851
BF = jnp.bfloat16
F32 = jnp.float32
MESH = pl.DeviceIdType.MESH


def gelu_all(u):
    t = jnp.tanh(u)
    s = 0.5 * t + 0.5
    return (u * s) * (1.0 / HALF_SLOPE), s + u * (0.5 - 0.5 * t * t)


def colsum(v):
    return jnp.sum(v.reshape(v.shape[0] // 8, 8, v.shape[1]), axis=0)


def squash(v):
    return jnp.sum(v, axis=0, keepdims=True)


class Kernel:
    def __init__(self, mesh, rows, channels, hidden, packed):
        self.ndp, self.nsub = mesh.shape["dp"], mesh.shape["sub"]
        self.rows, self.C, self.H = rows, channels, hidden
        self.packed = packed
        self.total = rows * self.ndp * self.nsub
        self.chips = self.ndp * self.nsub // 2
        self.nz = self.ndp // 2
        self.cw, self.hw = channels // self.ndp, hidden // self.nsub

    def scratch(self):
        R, C, H = self.rows, self.C, self.H
        V, D = pltpu.VMEM, pltpu.SemaphoreType.DMA
        s = dict(
            x=V((R, C), BF),
            og=V((R, C), BF),
            act=V((R, C), BF),
            slope=V((R, C), BF),
            big=V((R + 2 * PAD, 3 * H), F32),
            conv=V((R, H), F32),
            p2g=V((R, H), F32),
            act2=V((R, H), BF),
            bg=V((R, C), BF),
            back=V((R, 3 * H), BF),
            outv=V((R, C), BF),
            mb=V((R, 128), F32),
            ma=V((R, 128), F32),
            hs=V((2, PAD, H), F32),
            hc=V((2, PAD, H), F32),
            acc1=V((2, 8, C), F32),
            acc2=V((2, 8, H), F32),
            c1=V((2, 2, C), F32),
            c2=V((2, 2, H), F32),
            c3=V((2, 2, H), F32),
            c4=V((2, 2, C), F32),
            s1=V((self.chips, 2, C), F32),
            s2=V((self.chips, 2, H), F32),
            s3=V((self.chips, 2, H), F32),
            s4=V((self.chips, 2, C), F32),
            ar_send=D((4, 2)),
            ar_recv=D((4, 2)),
            xsem=D((4,)),
            ogsem=D,
            osem=D((8,)),
            isem=D((8,)),
            halo_send=D((2, 2)),
            halo_recv=D((2, 2)),
        )
        if self.packed:
            nz, n = self.nz, self.cw
            s.update(
                wf=V((C, 3 * H), BF),
                pf=V((H, C), BF),
                g=V((3, 2, 2, 2, nz, n, 128), BF),
                ag_send=D((3, 3)),
                ag_z=D((3,)),
                ag_xy=D((3, 3)),
                ag_core=D((3, 4)),
                rs=V((3, 2, 2, 2, nz, n, 128), BF),
                rc=V((3, 2, 2, nz, n, 128), BF),
                rd=V((3, nz, n, 128), BF),
                rxy=V((3, 2, nz, n, 128), BF),
                rz=V((3, nz, n, 128), BF),
                rs_send=D((3, 4)),
                rs_core=D((3,)),
                rs_d=D((3,)),
                rs_xy=D((3, 2)),
                rs_z=D((3,)),
            )
        return s

    def place(self):
        self.dp, self.sub = lax.axis_index("dp"), lax.axis_index("sub")
        self.z, self.y = self.dp // 2, lax.rem(self.dp, 2)
        self.x, self.c = self.sub // 2, lax.rem(self.sub, 2)
        n = self.ndp * self.nsub
        me = self.dp * self.nsub + self.sub
        nxt, prv = lax.rem(me + 1, n), lax.rem(me + n - 1, n)
        self.core_nbr = (self.dp, self.x * 2 + 1 - self.c)
        self.x_nbr = (self.dp, (self.nsub // 2 - 1 - self.x) * 2 + self.c)
        self.y_nbr = (self.z * 2 + 1 - self.y, self.sub)
        self.next = (nxt // self.nsub, lax.rem(nxt, self.nsub))
        self.prev = (prv // self.nsub, lax.rem(prv, self.nsub))
        self.chip = self.dp * (self.nsub // 2) + self.x

    def chip_device(self, chip):
        half = self.nsub // 2
        return (chip // half, lax.rem(chip, half) * 2 + self.c)

    def z_device(self, d):
        return (lax.rem(self.z + d, self.nz) * 2 + self.y, self.sub)

    def greet(self):
        b = pltpu.get_barrier_semaphore()

        def hello(device):
            pl.semaphore_signal(b, inc=1, device_id=device, device_id_type=MESH)

        hello(self.core_nbr)
        n = self.ndp * self.nsub
        me = self.dp * self.nsub + self.sub
        far = lax.rem(me + jnp.where(self.c == 1, 1, n - 1), n)
        hello((far // self.nsub, lax.rem(far, self.nsub)))

        def one(d, carry):
            hello(self.chip_device(lax.rem(self.chip + d, self.chips)))
            return carry

        lax.fori_loop(1, self.chips, one, 0)

    def greeted(self):
        pl.semaphore_wait(pltpu.get_barrier_semaphore(), self.chips + 1)

    def copy_to(self, src, dst, send, recv, device):
        return pltpu.make_async_remote_copy(
            src, dst, send, recv, device_id=device, device_id_type=MESH
        )

    def ar_begin(self, r, i, top, low):
        cs = (r.c1, r.c2, r.c3, r.c4)[i]
        cs[self.c, 0:1, :] = top
        cs[self.c, 1:2, :] = low
        mine = cs.at[self.c]
        self.copy_to(mine, mine, r.ar_send.at[i, 0], r.ar_recv.at[i, 0], self.core_nbr).start()

    def ar_middle(self, r, i):
        cs, sl = (r.c1, r.c2, r.c3, r.c4)[i], (r.s1, r.s2, r.s3, r.s4)[i]
        pltpu.make_async_copy(cs.at[0], cs.at[0], r.ar_recv.at[i, 0]).wait()
        sl[self.chip] = cs[0] + cs[1]
        mine = sl.at[self.chip]

        def one(d, carry):
            device = self.chip_device(lax.rem(self.chip + d, self.chips))
            self.copy_to(mine, mine, r.ar_send.at[i, 1], r.ar_recv.at[i, 1], device).start()
            return carry

        lax.fori_loop(1, self.chips, one, 0)

    def ar_end(self, r, i):
        sl = (r.s1, r.s2, r.s3, r.s4)[i]
        most = sl.at[pl.ds(0, self.chips - 1)]
        pltpu.make_async_copy(most, most, r.ar_recv.at[i, 1]).wait()
        if self.chips <= 16:
            total = sl[0]
            for k in range(1, self.chips):
                total = total + sl[k]
        else:
            total = lax.fori_loop(1, self.chips, lambda k, t: t + sl[k], sl[0])
        return total[0:1, :], total[1:2, :]

    def ar_drain(self, r, i):
        cs, sl = (r.c1, r.c2, r.c3, r.c4)[i], (r.s1, r.s2, r.s3, r.s4)[i]
        pltpu.make_async_copy(cs.at[0], cs.at[0], r.ar_send.at[i, 0]).wait()
        most = sl.at[pl.ds(0, self.chips - 1)]
        pltpu.make_async_copy(most, most, r.ar_send.at[i, 1]).wait()

    def mine(self, r, k):
        return r.g.at[k, self.y, self.x, self.c]

    def ag_start(self, r, conv, point):
        for k in range(3):
            r.g[k, self.y, self.x, self.c, self.z] = jnp.concatenate(
                [conv[k], point[:, 32 * k : 32 * k + 32]], axis=1
            )
            slot = r.g.at[k, self.y, self.x, self.c, self.z]
            for d in range(1, self.nz):
                self.copy_to(slot, slot, r.ag_send.at[k, 0], r.ag_z.at[k], self.z_device(d)).start()

    def to_core(self, r, k, j, grp):
        self.copy_to(grp, grp, r.ag_send.at[k, 2], r.ag_core.at[k, j], self.core_nbr).start()

    def ag_plane(self, r, k):
        grp = self.mine(r, k)
        part = grp.at[pl.ds(0, self.nz - 1)]
        pltpu.make_async_copy(part, part, r.ag_z.at[k]).wait()
        self.copy_to(grp, grp, r.ag_send.at[k, 1], r.ag_xy.at[k, 0], self.y_nbr).start()
        self.copy_to(grp, grp, r.ag_send.at[k, 1], r.ag_xy.at[k, 1], self.x_nbr).start()
        self.to_core(r, k, 0, grp)

    def ag_diagonal(self, r, k):
        by_y = r.g.at[k, 1 - self.y, self.x, self.c]
        by_x = r.g.at[k, self.y, 1 - self.x, self.c]
        first, second = (by_y, by_x) if k % 2 == 0 else (by_x, by_y)
        f, s = (0, 1) if k % 2 == 0 else (1, 0)
        to = self.x_nbr if k % 2 == 0 else self.y_nbr
        pltpu.make_async_copy(first, first, r.ag_xy.at[k, f]).wait()
        self.copy_to(first, first, r.ag_send.at[k, 1], r.ag_xy.at[k, 2], to).start()
        self.to_core(r, k, 1, first)
        pltpu.make_async_copy(second, second, r.ag_xy.at[k, s]).wait()
        self.to_core(r, k, 2, second)

    def ag_last(self, r, k):
        grp = r.g.at[k, 1 - self.y, 1 - self.x, self.c]
        pltpu.make_async_copy(grp, grp, r.ag_xy.at[k, 2]).wait()
        self.to_core(r, k, 3, grp)

    def ag_unpack(self, r, k):
        for j in range(4):
            grp = self.mine(r, k)
            pltpu.make_async_copy(grp, grp, r.ag_core.at[k, j]).wait()
        n, H = self.cw, self.H
        for z in range(self.nz):
            for y in range(2):
                dp = z * 2 + y
                parts = [r.g[k, y, s // 2, s % 2, z] for s in range(4)]
                r.wf[dp * n : dp * n + n, k * H : k * H + H] = jnp.concatenate(
                    [p[:, 0:96] for p in parts], axis=1
                )
                for s in range(4):
                    at = dp * n + 32 * k
                    r.pf[s * 96 : s * 96 + 96, at : at + 32] = parts[s][:, 96:128]

    def ag_drain(self, r):
        for k in range(3):
            grp = self.mine(r, k)
            part = grp.at[pl.ds(0, self.nz - 1)]
            pltpu.make_async_copy(part, part, r.ag_send.at[k, 0]).wait()
            for _ in range(3):
                pltpu.make_async_copy(grp, grp, r.ag_send.at[k, 1]).wait()
            for _ in range(4):
                pltpu.make_async_copy(grp, grp, r.ag_send.at[k, 2]).wait()

    def rs_core(self, r, k):
        for y in range(2):
            for x in range(2):
                self.copy_to(
                    r.rs.at[k, y, x, 1 - self.c],
                    r.rc.at[k, y, x],
                    r.rs_send.at[k, 0],
                    r.rs_core.at[k],
                    self.core_nbr,
                ).start()

    def add(self, r, k, y, x, *others):
        for z in range(self.nz):
            v = r.rs[k, y, x, self.c, z].astype(F32)
            for o in others:
                v = v + o[z].astype(F32)
            r.rs[k, y, x, self.c, z] = v.astype(BF)

    def rs_diagonal(self, r, k):
        pltpu.make_async_copy(r.rc.at[k], r.rc.at[k], r.rs_core.at[k]).wait()
        for y in range(2):
            for x in range(2):
                self.add(r, k, y, x, r.rc.at[k, y, x])
        to = self.x_nbr if k % 2 == 0 else self.y_nbr
        src = r.rs.at[k, 1 - self.y, 1 - self.x, self.c]
        self.copy_to(src, r.rd.at[k], r.rs_send.at[k, 1], r.rs_d.at[k], to).start()

    def rs_plane(self, r, k):
        pltpu.make_async_copy(r.rd.at[k], r.rd.at[k], r.rs_d.at[k]).wait()
        if k % 2 == 0:
            self.add(r, k, 1 - self.y, self.x, r.rd.at[k])
        else:
            self.add(r, k, self.y, 1 - self.x, r.rd.at[k])
        by_y = r.rs.at[k, 1 - self.y, self.x, self.c]
        by_x = r.rs.at[k, self.y, 1 - self.x, self.c]
        self.copy_to(by_y, r.rxy.at[k, 0], r.rs_send.at[k, 2], r.rs_xy.at[k, 0], self.y_nbr).start()
        self.copy_to(by_x, r.rxy.at[k, 1], r.rs_send.at[k, 2], r.rs_xy.at[k, 1], self.x_nbr).start()

    def rs_column(self, r, k):
        for j in range(2):
            pltpu.make_async_copy(r.rxy.at[k, j], r.rxy.at[k, j], r.rs_xy.at[k, j]).wait()
        self.add(r, k, self.y, self.x, r.rxy.at[k, 0], r.rxy.at[k, 1])
        for d in range(1, self.nz):
            to = lax.rem(self.z + d, self.nz)
            src = r.rs.at[k, self.y, self.x, self.c, to]
            self.copy_to(src, r.rz.at[k, self.z], r.rs_send.at[k, 3], r.rs_z.at[k], self.z_device(d)).start()
        r.rz[k, self.z] = r.rs[k, self.y, self.x, self.c, self.z]

    def rs_end(self, r, k):
        part = r.rz.at[k, pl.ds(0, self.nz - 1)]
        pltpu.make_async_copy(part, part, r.rs_z.at[k]).wait()
        v = r.rz[k, 0].astype(F32)
        for z in range(1, self.nz):
            v = v + r.rz[k, z].astype(F32)
        r.conv_grad[k] = v[:, 0:96]
        r.point_grad[:, 32 * k : 32 * k + 32] = v[:, 96:128]

    def rs_drain(self, r):
        for k in range(3):
            grp = r.rd.at[k]
            pltpu.make_async_copy(r.rc.at[k], r.rc.at[k], r.rs_send.at[k, 0]).wait()
            pltpu.make_async_copy(grp, grp, r.rs_send.at[k, 1]).wait()
            for _ in range(2):
                pltpu.make_async_copy(grp, grp, r.rs_send.at[k, 2]).wait()
            part = r.rz.at[k, pl.ds(0, self.nz - 1)]
            pltpu.make_async_copy(part, part, r.rs_send.at[k, 3]).wait()

    def halo_begin(self, r, i, low_lanes, high_lanes):
        R, H = self.rows, self.H
        buf = r.hs if i == 0 else r.hc
        wide = lambda m: jnp.concatenate([m] * (H // 128), axis=1)
        buf[0] = r.big[PAD : 2 * PAD, low_lanes : low_lanes + H] * wide(r.mb[0:PAD])
        buf[1] = r.big[R : R + PAD, high_lanes : high_lanes + H] * wide(r.ma[R - PAD : R])
        self.copy_to(
            buf.at[0], r.halo.at[i, 0], r.halo_send.at[i, 0], r.halo_recv.at[i, 0], self.prev
        ).start()
        self.copy_to(
            buf.at[1], r.halo.at[i, 1], r.halo_send.at[i, 1], r.halo_recv.at[i, 1], self.next
        ).start()

    def halo_end(self, r, i, low_lanes, high_lanes):
        R, H = self.rows, self.H
        for j in range(2):
            pltpu.make_async_copy(r.halo.at[i, j], r.halo.at[i, j], r.halo_recv.at[i, j]).wait()
        r.big[R + PAD : R + 2 * PAD, low_lanes : low_lanes + H] = r.halo[i, 0]
        r.big[0:PAD, high_lanes : high_lanes + H] = r.halo[i, 1]

    def halo_drain(self, r, i):
        for j in range(2):
            pltpu.make_async_copy(r.halo.at[i, j], r.halo.at[i, j], r.halo_send.at[i, j]).wait()


def loop(rows, tile, f):
    def one(i, carry):
        f(pl.multiple_of(i * tile, tile))
        return carry

    lax.fori_loop(0, rows // tile, one, 0)


def row_tile(start, tile):
    return start + lax.broadcasted_iota(jnp.int32, (tile, 128), 0)


def wide(m, n):
    return jnp.concatenate([m] * (n // 128), axis=1)


class Refs:
    pass


def kernel(k, n_in, n_out, names, *refs):
    r = Refs()
    ins, outs, scr = refs[:n_in], refs[n_in : n_in + n_out], refs[n_in + n_out :]
    for name, ref in zip(names, scr):
        setattr(r, name, ref)
    (x_hbm, og_hbm, species, first, sw, conv_w, point_w, g1, b1, g2, b2, run1, run2) = ins
    (out_hbm, ig_hbm, r.conv_grad, r.point_grad, gg1, gb1, gg2, gb2, new1, new2) = outs
    R, C, H, N = k.rows, k.C, k.H, k.total
    k.place()
    k.greet()
    Q = R // 4
    xcopies = [
        pltpu.make_async_copy(x_hbm.at[pl.ds(q * Q, Q)], r.x.at[pl.ds(q * Q, Q)], r.xsem.at[q])
        for q in range(4)
    ]
    for cp in xcopies:
        cp.start()
    ogcopy = pltpu.make_async_copy(og_hbm, r.og, r.ogsem)
    ogcopy.start()
    k.greeted()
    if k.packed:
        k.ag_start(r, conv_w, point_w)

    r.acc1[...] = jnp.zeros_like(r.acc1)
    for q in range(4):
        xcopies[q].wait()
        v = r.x[q * Q : q * Q + Q, :].astype(F32)
        r.acc1[0] += colsum(v)
        r.acc1[1] += colsum(v * v)
    k.ar_begin(r, 0, squash(r.acc1[0]), squash(r.acc1[1]))

    fs = first[0]
    starts = [fs + SEQ_LEN * j for j in range(R // SEQ_LEN)]

    def masks(at):
        row = row_tile(at, 128)
        before = jnp.ones((128, 128), F32)
        after = jnp.ones((128, 128), F32)
        for s in starts:
            before = jnp.where((row >= s) & (row < s + DIL), 0.0, before)
            after = jnp.where((row >= s - DIL) & (row < s), 0.0, after)
        r.mb[pl.ds(at, 128), :] = before
        r.ma[pl.ds(at, 128), :] = after

    loop(R, 128, masks)
    k.ar_middle(r, 0)
    if k.packed:
        for j in range(3):
            k.ag_plane(r, j)
    sum1, sq1 = k.ar_end(r, 0)
    mean1 = sum1 / N
    var1 = sq1 / N - mean1 * mean1
    inv1 = lax.rsqrt(var1 + EPSILON)
    scale1 = (HALF_SLOPE * g1[...]) * inv1
    shift1 = HALF_SLOPE * b1[...] - mean1 * scale1

    def act_tile(at):
        rows = pl.ds(at, 256)
        a, s = gelu_all(r.x[rows, :].astype(F32) * scale1 + shift1)
        r.act[rows, :] = a.astype(BF)
        r.slope[rows, :] = s.astype(BF)

    loop(R, 256, act_tile)
    if k.packed:
        for j in range(3):
            k.ag_diagonal(r, j)
        for j in range(3):
            k.ag_last(r, j)
        for j in range(3):
            k.ag_unpack(r, j)
        wf, pf = r.wf, r.pf
    else:
        wf, pf = conv_w, point_w

    for at in (0, R - Q):
        r.big[PAD + at : PAD + at + Q, :] = jnp.dot(
            r.act[at : at + Q, :], wf[...], preferred_element_type=F32
        )
    k.halo_begin(r, 0, 2 * H, 0)
    for at in range(Q, R - Q, Q):
        r.big[PAD + at : PAD + at + Q, :] = jnp.dot(
            r.act[at : at + Q, :], wf[...], preferred_element_type=F32
        )
    k.halo_end(r, 0, 2 * H, 0)
    r.acc2[...] = jnp.zeros_like(r.acc2)
    T = 256

    def gather_taps(at):
        rows = pl.ds(at, T)
        lo = r.big[pl.ds(at, T + 2 * PAD), 0:H][PAD - DIL : PAD - DIL + T]
        mid = r.big[pl.ds(at + PAD, T), H : 2 * H]
        hi = r.big[pl.ds(at, T + 2 * PAD), 2 * H : 3 * H][PAD + DIL : PAD + DIL + T]
        v = lo * wide(r.mb[rows, :], H) + mid + hi * wide(r.ma[rows, :], H)
        r.conv[rows, :] = v
        r.acc2[0] += colsum(v)
        r.acc2[1] += colsum(v * v)

    loop(R, T, gather_taps)
    k.ar_begin(r, 1, squash(r.acc2[0]), squash(r.acc2[1]))
    k.ar_middle(r, 1)

    ogcopy.wait()
    at_start = [species[0]] + [species[s] for s in starts]
    weights = [jnp.where(sp == 0, sw[0:1, :], sw[1:2, :]) for sp in at_start]

    def row_weight(at, tile):
        row = row_tile(at, tile)
        w = jnp.broadcast_to(weights[0], (tile, C))
        for s, v in zip(starts, weights[1:]):
            w = jnp.where(wide(row, C) >= s, v, w)
        return w

    def branch_grad(at):
        rows = pl.ds(at, 128)
        r.bg[rows, :] = (r.og[rows, :].astype(F32) * row_weight(at, 128)).astype(BF)

    loop(R, 128, branch_grad)

    def act_two_grad(at):
        rows = pl.ds(at, 1024)
        r.p2g[rows, :] = lax.dot_general(
            r.bg[rows, :], pf[...], (((1,), (1,)), ((), ())), preferred_element_type=F32
        )

    loop(R, 1024, act_two_grad)
    sum2, sq2 = k.ar_end(r, 1)
    mean2 = sum2 / N
    var2 = sq2 / N - mean2 * mean2
    inv2 = lax.rsqrt(var2 + EPSILON)
    minv2 = mean2 * inv2
    gain2, bias2 = HALF_SLOPE * g2[...], HALF_SLOPE * b2[...]
    r.acc2[...] = jnp.zeros_like(r.acc2)

    def second_norm(at):
        rows = pl.ds(at, 256)
        zh = r.conv[rows, :] * inv2 - minv2
        a, s = gelu_all(zh * gain2 + bias2)
        r.act2[rows, :] = a.astype(BF)
        p = r.p2g[rows, :] * s
        r.p2g[rows, :] = p
        r.acc2[0] += colsum(p)
        r.acc2[1] += colsum(p * zh)

    loop(R, 256, second_norm)
    k.ar_begin(r, 2, squash(r.acc2[0]), squash(r.acc2[1]))
    k.ar_middle(r, 2)

    ocopies = []
    for q in range(2):
        rows = pl.ds(q * 1024, 1024)
        br = jnp.dot(r.act2[rows, :], pf[...], preferred_element_type=F32)
        r.outv[rows, :] = (r.x[rows, :].astype(F32) + br).astype(BF)
        cp = pltpu.make_async_copy(r.outv.at[rows], out_hbm.at[rows], r.osem.at[q])
        cp.start()
        ocopies.append(cp)
    pg = lax.dot_general(
        r.act2[...], r.bg[...], (((0,), (0,)), ((), ())), preferred_element_type=F32
    )
    if k.packed:
        pgb = pg.astype(BF)
        for j in range(3):
            for z in range(k.nz):
                for y in range(2):
                    for s in range(4):
                        lane = (z * 2 + y) * 96 + 32 * j
                        r.rs[j, y, s // 2, s % 2, z, :, 96:128] = pgb[
                            s * 96 : s * 96 + 96, lane : lane + 32
                        ]
    else:
        r.point_grad[...] = pg
    bsum, gsum = k.ar_end(r, 2)
    gb2[...] = bsum
    gg2[...] = gsum
    a2 = inv2 * g2[...]
    lin2 = -a2 * (gsum / N) * inv2
    off2 = -a2 * (bsum / N) + a2 * (gsum / N) * minv2

    def cot(at):
        rows = pl.ds(at, 256)
        r.big[pl.ds(at + PAD, 256), 0:H] = (
            r.p2g[rows, :] * a2 + r.conv[rows, :] * lin2 + off2
        )

    loop(R, 256, cot)
    k.halo_begin(r, 1, 0, 0)
    k.halo_end(r, 1, 0, 0)
    T2 = 128

    def shifted(at):
        rows = pl.ds(at, T2)
        v = r.big[pl.ds(at, T2 + 2 * PAD), 0:H]
        r.back[rows, 0:H] = (v[PAD + DIL : PAD + DIL + T2] * wide(r.ma[rows, :], H)).astype(BF)
        r.back[rows, H : 2 * H] = v[PAD : PAD + T2].astype(BF)
        r.back[rows, 2 * H : 3 * H] = (v[PAD - DIL : PAD - DIL + T2] * wide(r.mb[rows, :], H)).astype(BF)

    loop(R, T2, shifted)

    M = 384
    for m in range(0, C, M):
        cg = lax.dot_general(
            r.act[:, m : m + M], r.back[...], (((0,), (0,)), ((), ())), preferred_element_type=F32
        )
        if k.packed:
            cgb = cg.astype(BF)
            for j in range(3):
                for d in range(M // 96):
                    dp = m // 96 + d
                    for s in range(4):
                        lane = j * H + s * 96
                        r.rs[j, dp % 2, s // 2, s % 2, dp // 2, :, 0:96] = cgb[
                            d * 96 : d * 96 + 96, lane : lane + 96
                        ]
        else:
            for j in range(3):
                r.conv_grad[j, m : m + M, :] = cg[:, j * H : j * H + H]
    if k.packed:
        for j in range(3):
            k.rs_core(r, j)
        for j in range(3):
            k.rs_diagonal(r, j)

    minv1 = mean1 * inv1
    r.acc1[...] = jnp.zeros_like(r.acc1)
    for q in range(4):
        rows = slice(q * Q, q * Q + Q)
        ag = lax.dot_general(
            r.back[rows, :], wf[...], (((1,), (1,)), ((), ())), preferred_element_type=F32
        )
        p = ag * r.slope[rows, :].astype(F32)
        r.big[rows, 0:C] = p
        r.acc1[0] += colsum(p)
        r.acc1[1] += colsum(p * (r.x[rows, :].astype(F32) * inv1 - minv1))
    k.ar_begin(r, 3, squash(r.acc1[0]), squash(r.acc1[1]))
    k.ar_middle(r, 3)
    if k.packed:
        for j in range(3):
            k.rs_plane(r, j)
    unbias = N / (N - 1.0)
    new1[0:1, :] = MOMENTUM * run1[0:1, :] + (1.0 - MOMENTUM) * mean1
    new1[1:2, :] = MOMENTUM * run1[1:2, :] + (1.0 - MOMENTUM) * (var1 * unbias)
    new2[0:1, :] = MOMENTUM * run2[0:1, :] + (1.0 - MOMENTUM) * mean2
    new2[1:2, :] = MOMENTUM * run2[1:2, :] + (1.0 - MOMENTUM) * (var2 * unbias)
    bsum1, gsum1 = k.ar_end(r, 3)
    gb1[...] = bsum1
    gg1[...] = gsum1
    a1 = inv1 * g1[...]
    lin1 = -a1 * (gsum1 / N) * inv1
    off1 = -a1 * (bsum1 / N) + a1 * (gsum1 / N) * minv1

    icopies = []
    for q in range(4):

        def last(at):
            rows = pl.ds(at, 128)
            v = r.og[rows, :].astype(F32) * row_weight(at, 128)
            v = v + r.big[rows, 0:C] * a1 + r.x[rows, :].astype(F32) * lin1 + off1
            r.og[rows, :] = v.astype(BF)

        lax.fori_loop(
            0, Q // 128, lambda i, c: (last(pl.multiple_of(q * Q + i * 128, 128)), c)[1], 0
        )
        rows = pl.ds(q * Q, Q)
        cp = pltpu.make_async_copy(r.og.at[rows], ig_hbm.at[rows], r.isem.at[q])
        cp.start()
        icopies.append(cp)
    if k.packed:
        for j in range(3):
            k.rs_column(r, j)
        for j in range(3):
            k.rs_end(r, j)
        k.ag_drain(r)
        k.rs_drain(r)
    for i in range(4):
        k.ar_drain(r, i)
    for i in range(2):
        k.halo_drain(r, i)
    for cp in ocopies + icopies:
        cp.wait()


def body(
    mesh,
    activations,
    out_grad,
    species,
    first_start,
    species_weight,
    conv_weight,
    point_weight,
    gain_one,
    bias_one,
    gain_two,
    bias_two,
    running_one,
    running_two,
):
    rows, C = activations.shape
    ndp, nsub = mesh.shape["dp"], mesh.shape["sub"]
    cw, hw = conv_weight.shape[1:]
    taps, H = conv_weight.shape[0], hw * nsub
    packed = cw == 96 and hw == 96 and nsub == 4 and ndp % 2 == 0
    if not packed:
        conv_weight = lax.all_gather(conv_weight, "dp", axis=1, tiled=True)
        conv_weight = lax.all_gather(conv_weight, "sub", axis=2, tiled=True)
        conv_weight = jnp.transpose(conv_weight, (1, 0, 2)).reshape(C, taps * H)
        point_weight = lax.all_gather(point_weight, "dp", axis=1, tiled=True)
        point_weight = lax.all_gather(point_weight, "sub", axis=0, tiled=True)
    k = Kernel(mesh, rows, C, H, packed)
    scratch = k.scratch()
    scratch["halo"] = pltpu.VMEM((2, 2, PAD, H), F32)
    any_, vmem, smem = (
        pl.BlockSpec(memory_space=pl.ANY),
        pl.BlockSpec(memory_space=pltpu.VMEM),
        pl.BlockSpec(memory_space=pltpu.SMEM),
    )
    row = lambda v: v.reshape(1, -1)
    sds = jax.ShapeDtypeStruct
    out_shape = (
        sds((rows, C), BF),
        sds((rows, C), BF),
        sds((taps, cw, hw) if packed else (taps, C, H), F32),
        sds((hw, cw) if packed else (H, C), F32),
        sds((1, C), F32),
        sds((1, C), F32),
        sds((1, H), F32),
        sds((1, H), F32),
        sds((2, C), F32),
        sds((2, H), F32),
    )
    outs = pl.pallas_call(
        functools.partial(kernel, k, 13, 10, list(scratch)),
        out_shape=out_shape,
        in_specs=[any_, any_, smem, smem] + [vmem] * 9,
        out_specs=[any_, any_] + [vmem] * 8,
        scratch_shapes=list(scratch.values()),
        compiler_params=pltpu.CompilerParams(
            collective_id=0, has_side_effects=True, vmem_limit_bytes=62 * 2**20
        ),
    )(
        activations,
        out_grad,
        species,
        first_start,
        species_weight,
        conv_weight,
        point_weight,
        row(gain_one),
        row(bias_one),
        row(gain_two),
        row(bias_two),
        running_one,
        running_two,
    )
    output, input_grad, conv_grad, point_grad, gg1, gb1, gg2, gb2, new1, new2 = outs
    if not packed:
        conv_grad = lax.psum_scatter(conv_grad, "dp", scatter_dimension=1, tiled=True)
        point_grad = lax.psum_scatter(point_grad, "dp", scatter_dimension=1, tiled=True)
        conv_grad = lax.psum_scatter(conv_grad, "sub", scatter_dimension=2, tiled=True)
        point_grad = lax.psum_scatter(point_grad, "sub", scatter_dimension=0, tiled=True)
    flat = lambda v: v.reshape(-1)
    return (
        output,
        input_grad,
        conv_grad,
        point_grad,
        flat(gg1),
        flat(gb1),
        flat(gg2),
        flat(gb2),
        new1,
        new2,
    )


def solution(mesh):
    in_specs = (
        P(("dp", "sub"), None),
        P(("dp", "sub"), None),
        P(("dp", "sub")),
        P(("dp", "sub")),
        P(),
        P(None, "dp", "sub"),
        P("sub", "dp"),
        P(),
        P(),
        P(),
        P(),
        P(),
        P(),
    )
    out_specs = (
        P(("dp", "sub"), None),
        P(("dp", "sub"), None),
        P(None, "dp", "sub"),
        P("sub", "dp"),
        P(),
        P(),
        P(),
        P(),
        P(),
        P(),
    )
    return jax.shard_map(
        functools.partial(body, mesh), mesh=mesh, in_specs=in_specs, out_specs=out_specs, check_vma=False
    )
```

time: 469 us -> 104 us (0.22)
  blocking collectives: 237 us -> 0 us
  waiting for transfers between devices: 105 us -> 0 us
  Pallas kernels: 0 us -> 83.9 us
  matrix products: 46.3 us -> 0 us
  other arithmetic: 29.3 us -> 5.07 us
  starting transfers between devices: 14.7 us -> 0 us
  between operations: 14.8 us -> 1.32 us
  local copies, waits for them, and re-layouts: 20.7 us -> 13.1 us
    psum x4 -> x0, blocking collectives: 159 us -> none  [the longest x1 41.2 us: body(): lax.psum((jnp.sum(pre_two_grad, axis=0), jnp.sum(pre_two_grad * z_hat, ax...]
    pallas_call x0 -> x1, Pallas kernels: none -> 83.9 us  [body(): pl.pallas_call(functools.partial(kernel, k, 13, 10, list(scratch)), out_s...]
    all_gather x3 -> x0, blocking collectives: 77.4 us -> none  [the longest x1 36 us: body(): lax.all_gather(conv_weight, 'dp', axis=1, tiled=True)]
    reduce_scatter x2 -> x0, waiting for transfers between devices: 68.3 us -> none  [the longest x1 57.1 us: body(): lax.psum_scatter(conv_grad, 'dp', scatter_dimension=1, tiled=True)]
    dot_general x6 -> x0, matrix products: 46.3 us -> none  [the longest x1 10.7 us: body(): jnp.dot(back_in, conv_back, preferred_element_type=jnp.float32)]
    unnamed x7 -> x0, waiting for transfers between devices: 36.3 us -> none
    ppermute x6 -> x0, starting transfers between devices: 14.3 us -> none  [the longest x3 10.4 us: padded(): lax.ppermute(lax.slice_in_dim(block, block.shape[dim] - width, None, axis...]
    convert_element_type x7 -> x0, other arithmetic: 14 us -> none  [the longest x1 6.23 us: body(): input_grad.astype(jnp.bfloat16)]
  transfers between devices with their start and end apart: 11 -> 0, of which waited for: 4 -> 0; matrix products, arithmetic and copies ran while one was open for 13% -> 0% of each run, Pallas kernels for 0% -> 0%
where the time goes in v1:
time: 104 us; the launch traced here: 103 us
  Pallas kernels  83.9 us (81%)
  local copies, waits for them, and re-layouts  13.1 us (13%)
  other arithmetic  5.07 us (5%)
  between operations  1.32 us (1%)
    pallas_call x1, Pallas kernels, body(): pl.pallas_call(functools.partial(kernel, k, 13, 10, list(scratch)), out_s...  83.9 us
    unnamed x16, local copies, waits for them, and re-layouts  8.04 us
    pallas_call x4, other arithmetic, body(): pl.pallas_call(functools.partial(kernel, k, 13, 10, list(scratch)), out_s...  5.07 us
    reshape x4, local copies, waits for them, and re-layouts, body(): row = lambda v: v.reshape(1, -1)  5.02 us

profile of v1, /device:TPU:0, one launch (start us, length us, event | category | flops | bytes accessed | tf_op | source)
XLA Modules:
  0.0 103.3 jit_solution(9706382391251926686)
XLA Ops:
  0.6 1.3 %reshape.44.refs_7_ = f32[1,768]{1,0:T(1,128)} reshape(f32[768]{0:T(1024)} %param.20) | data formatting | bytes 6144 | tf_op jit(solution)/shard_map/reshape | solution.py:684
  1.9 1.3 %reshape.45.refs_8_ = f32[1,768]{1,0:T(1,128)} reshape(f32[768]{0:T(1024)} %param.21) | data formatting | bytes 6144 | tf_op jit(solution)/shard_map/reshape | solution.py:684
  3.2 1.2 %reshape.46.refs_9_ = f32[1,384]{1,0:T(1,128)} reshape(f32[384]{0:T(512)} %param.22) | data formatting | bytes 3072 | tf_op jit(solution)/shard_map/reshape | solution.py:684
  4.4 1.2 %reshape.47.refs_10_ = f32[1,384]{1,0:T(1,128)} reshape(f32[384]{0:T(512)} %param.23) | data formatting | bytes 3072 | tf_op jit(solution)/shard_map/reshape | solution.py:684
  6.3 83.9 %shard_map.204 = (bf16[2048,768]{1,0:T(8,128)(2,1)}, bf16[2048,768]{1,0:T(8,128)(2,1)}, f32[3,96,96]{2,1,0:T(8,128)}, f32[96,96]{1,0:T(8,128)}, f32[1,768]{1,0:T...) custom-call(bf16[2048,768]{1,0:T(8,128)(2,1)} %refs_0_.1, ...), custom_call_target="tpu_custom_call" | custom-call | tf_op jit(solution)/shard_map/pallas_call | solution.py:698
  90.2 1.3 %reduce = f32[768]{0:T(1024)} reduce(f32[1,768]{1,0:T(1,128)} %get-tuple-element.24, f32[]{:T(128)} %constant.1), dimensions={0}, to_apply=%get-tuple-element.24.reduce_sub_computation | reduce | bytes 6148 | tf_op jit(solution)/shard_map/pallas_call | solution.py:698
  91.5 1.3 %reduce.1 = f32[768]{0:T(1024)} reduce(f32[1,768]{1,0:T(1,128)} %get-tuple-element.25, f32[]{:T(128)} %constant.1), dimensions={0}, to_apply=%get-tuple-element.25.reduce_sub_computation | reduce | bytes 6148 | tf_op jit(solution)/shard_map/pallas_call | solution.py:698
  92.7 1.3 %reduce.2 = f32[384]{0:T(512)} reduce(f32[1,384]{1,0:T(1,128)} %get-tuple-element.26, f32[]{:T(128)} %constant.1), dimensions={0}, to_apply=%get-tuple-element.26.reduce_sub_computation | reduce | bytes 3076 | tf_op jit(solution)/shard_map/pallas_call | solution.py:698
  94.0 1.3 %reduce.3 = f32[384]{0:T(512)} reduce(f32[1,384]{1,0:T(1,128)} %get-tuple-element.27, f32[]{:T(128)} %constant.1), dimensions={0}, to_apply=%get-tuple-element.27.reduce_sub_computation | reduce | bytes 3076 | tf_op jit(solution)/shard_map/pallas_call | solution.py:698
  95.3 0.0 copy-start
  95.3 3.9 %copy.30 = bf16[2048,768]{1,0:T(8,128)(2,1)} copy(bf16[2048,768]{1,0:T(8,128)(2,1)} %get-tuple-element.40) | data formatting | bytes 6291456
  99.2 0.0 copy-done
  99.2 0.0 copy-start.1
  99.2 0.0 copy-start.2
  99.2 0.0 copy-start.3
  99.2 0.0 copy-start.4
  99.2 1.7 %copy.31 = bf16[2048,768]{1,0:T(8,128)(2,1)} copy(bf16[2048,768]{1,0:T(8,128)(2,1)S(1)} %copy-done) | data formatting | bytes 6291456
  100.8 0.0 copy-done.1
  100.9 0.7 copy.32
  101.5 0.0 copy-done.2
  101.5 0.6 copy.33
  102.1 0.0 copy-done.3
  102.1 0.6 copy.34
  102.7 0.0 copy-done.4
  102.7 0.6 copy.35
Async XLA Ops:
  95.3 3.9 %copy-start = (bf16[2048,768]{1,0:T(8,128)(2,1)S(1)}, bf16[2048,768]{1,0:T(8,128)(2,1)}, u32[]{:S(2)}) copy-start(bf16[2048,768]{1,0:T(8,128)(2,1)} %get-tuple-element.41) | copy-start | bytes 9437188
  99.2 1.7 %copy-start.1 = (f32[3,96,96]{2,1,0:T(8,128)S(1)}, f32[3,96,96]{2,1,0:T(8,128)}, u32[]{:S(2)}) copy-start(f32[3,96,96]{2,1,0:T(8,128)} %get-tuple-element.42) | copy-start | bytes 331780
  99.2 2.4 %copy-start.2 = (f32[96,96]{1,0:T(8,128)S(1)}, f32[96,96]{1,0:T(8,128)}, u32[]{:S(2)}) copy-start(f32[96,96]{1,0:T(8,128)} %get-tuple-element.43) | copy-start | bytes 110596
  99.2 3.0 %copy-start.3 = (f32[2,768]{1,0:T(2,128)S(1)}, f32[2,768]{1,0:T(2,128)}, u32[]{:S(2)}) copy-start(f32[2,768]{1,0:T(2,128)} %get-tuple-element.48) | copy-start | bytes 18436
  99.2 3.6 %copy-start.4 = (f32[2,384]{1,0:T(2,128)S(1)}, f32[2,384]{1,0:T(2,128)}, u32[]{:S(2)}) copy-start(f32[2,384]{1,0:T(2,128)} %get-tuple-element.49) | copy-start | bytes 9220

commit v2 on v1

v2 whole, which is shorter than its diff:
```python
import functools

import jax
import jax.numpy as jnp
from jax import lax
from jax.experimental import pallas as pl
from jax.experimental.pallas import tpu as pltpu
from jax.sharding import PartitionSpec as P

DIL = 11
SEQ_LEN = 1024
EPSILON = 0.001
MOMENTUM = 0.9
PAD = 16
HALF_SLOPE = 0.851
BF = jnp.bfloat16
F32 = jnp.float32
MESH = pl.DeviceIdType.MESH
PARTS = ((0, 48), (48, 48), (96, 48), (144, 48), (192, 32), (224, 80))
CONV_ROWS, SLOT_ROWS = 224, 304
SIDE = 112


def gelu_all(u):
    t = jnp.tanh(u)
    s = 0.5 * t + 0.5
    return (u * s) * (1.0 / HALF_SLOPE), s + u * (0.5 - 0.5 * t * t)


def colsum(v):
    return jnp.sum(v.reshape(v.shape[0] // 8, 8, v.shape[1]), axis=0)


def squash(v):
    return jnp.sum(v, axis=0, keepdims=True)


def loop(first, last, tile, f):
    def one(i, carry):
        f(pl.multiple_of(first + i * tile, tile))
        return carry

    lax.fori_loop(0, (last - first) // tile, one, 0)


def row_tile(start, tile):
    return start + lax.broadcasted_iota(jnp.int32, (tile, 128), 0)


def wide(m, n):
    return jnp.concatenate([m] * (n // 128), axis=1)


class Kernel:
    def __init__(self, mesh, rows, channels, hidden, packed):
        self.ndp, self.nsub = mesh.shape["dp"], mesh.shape["sub"]
        self.rows, self.C, self.H = rows, channels, hidden
        self.packed = packed
        self.total = rows * self.ndp * self.nsub
        self.chips = self.ndp * self.nsub // 2
        self.nz = self.ndp // 2
        self.cw, self.hw = channels // self.ndp, hidden // self.nsub
        self.half = self.cw // 2
        self.sent, self.coming, self.local = [], {}, {}

    def scratch(self):
        R, C, H = self.rows, self.C, self.H
        V, D = pltpu.VMEM, pltpu.SemaphoreType.DMA
        s = dict(
            x=V((R, C), BF),
            og=V((R, C), BF),
            act=V((R, C), BF),
            slope=V((R, C), BF),
            big=V((R + 2 * PAD, 3 * H), F32),
            conv=V((R, H), F32),
            p2g=V((R, H), F32),
            act2=V((R, H), BF),
            back=V((R, 3 * H), BF),
            mb=V((R, 128), F32),
            ma=V((R, 128), F32),
            hs=V((2, PAD, H), F32),
            halo=V((2, PAD, H), F32),
            es=V((2, PAD, 2 * H + 128), F32),
            edge=V((2, PAD, 2 * H + 128), F32),
            acc1=V((2, 8, C), F32),
            acc2=V((2, 8, H), F32),
            c0=V((2, 2, C), F32),
            c1=V((2, 2, H), F32),
            c2=V((2, 2, H), F32),
            c3=V((2, 2, C), F32),
            s0=V((self.chips, 2, C), F32),
            s1=V((self.chips, 2, H), F32),
            s2=V((self.chips, 2, H), F32),
            s3=V((self.chips, 2, C), F32),
            wf=V((C, 3 * H), BF),
            pf=V((H, C), BF),
            sw=V((2, C), F32),
            g1=V((C,), F32),
            b1=V((C,), F32),
            g2=V((H,), F32),
            b2=V((H,), F32),
            run1=V((2, C), F32),
            run2=V((2, H), F32),
            species=pltpu.SMEM((R,), jnp.int32),
            first=pltpu.SMEM((1,), jnp.int32),
            ar_send=D((4, 2)),
            ar_recv=D((4, 2)),
            insem=D((24,)),
            halo_send=D((2, 2)),
            halo_recv=D((2, 2)),
        )
        if self.packed:
            nz = self.nz
            s.update(
                cshard=V((3, self.cw, self.hw), BF),
                pshard=V((self.hw, self.cw), BF),
                ag_send=D((len(PARTS), 3)),
                ag_z=D((len(PARTS),)),
                ag_own=D((len(PARTS), 2)),
                ag_oth=D((len(PARTS), 2)),
                ag_d=D((len(PARTS),)),
                ag_core=D((len(PARTS), 4)),
                ra=V((2, 2, 2, 2, 2, SIDE, 128), F32),
                rs=V((2, 2, 2, 2, 2, SIDE, 128), BF),
                rc=V((2, 2, 2, 2, 2, SIDE, 128), BF),
                st=V((2, 2, 2, 2, 2, SIDE, 128), BF),
                rd=V((2, 2, 2, SIDE, 128), BF),
                rxy=V((2, 2, 2, 2, SIDE, 128), BF),
                rz=V((2, 3, SIDE, 128), BF),
                rs_send=D((2, 2, 3)),
                rs_core=D((2, 2)),
                rs_d=D((2, 2)),
                rs_xy=D((2, 2, 2)),
                rz_send=D((2,)),
                rs_z=D((2,)),
                pa=V((2, 2, nz, 80, 128), F32),
                ps=V((2, 2, nz, 80, 128), BF),
                pc=V((2, 2, nz, 80, 128), BF),
                pt=V((2, 2, nz, 80, 128), BF),
                pd=V((nz, 80, 128), BF),
                pxy=V((2, nz, 80, 128), BF),
                pz=V((3, 80, 128), BF),
                p_send=D((4,)),
                p_recv=D((5,)),
            )
            s.update({f"w{j}": V((2, 2, 2, nz, n, 128), BF) for j, (_, n) in enumerate(PARTS)})
        return s

    def place(self):
        self.dp, self.sub = lax.axis_index("dp"), lax.axis_index("sub")
        self.z, self.y = self.dp // 2, lax.rem(self.dp, 2)
        self.x, self.c = self.sub // 2, lax.rem(self.sub, 2)
        n = self.ndp * self.nsub
        me = self.dp * self.nsub + self.sub
        nxt, prv = lax.rem(me + 1, n), lax.rem(me + n - 1, n)
        far = lax.rem(me + jnp.where(self.c == 1, 1, n - 1), n)
        self.core_nbr = (self.dp, self.x * 2 + 1 - self.c)
        self.x_nbr = (self.dp, (1 - self.x) * 2 + self.c)
        self.y_nbr = (self.z * 2 + 1 - self.y, self.sub)
        self.next = (nxt // self.nsub, lax.rem(nxt, self.nsub))
        self.prev = (prv // self.nsub, lax.rem(prv, self.nsub))
        self.far = (far // self.nsub, lax.rem(far, self.nsub))
        self.chip = self.dp * (self.nsub // 2) + self.x

    def z_device(self, d):
        return (lax.rem(self.z + d, self.nz) * 2 + self.y, self.sub)

    def each_chip(self, f):
        if self.chips == 16 and self.nsub == 4:
            z, y, x = self.z, self.y, self.x
            zs = (z, z + 1 - 2 * lax.rem(z, 2), lax.rem(z + 2, 4), 3 - z)
            for d in range(15, 0, -1):
                yy = 1 - y if (d // 2) % 2 else y
                xx = 1 - x if d % 2 else x
                f((zs[d // 4] * 2 + yy, xx * 2 + self.c))
        else:
            side = self.nsub // 2

            def one(d, carry):
                chip = lax.rem(self.chip + d, self.chips)
                f((chip // side, lax.rem(chip, side) * 2 + self.c))
                return carry

            lax.fori_loop(1, self.chips, one, 0)

    def greet(self):
        b = pltpu.get_barrier_semaphore()

        def hello(device):
            pl.semaphore_signal(b, inc=1, device_id=device, device_id_type=MESH)

        self.each_chip(hello)
        hello(self.far)
        hello(self.core_nbr)

    def greeted(self):
        pl.semaphore_wait(pltpu.get_barrier_semaphore(), self.chips + 1)

    def put(self, src, dst, send, recv, device, key=None, ref=None):
        pltpu.make_async_remote_copy(
            src, dst, send, recv, device_id=device, device_id_type=MESH
        ).start()
        self.sent.append((src, send))
        if key is not None:
            self.coming[key] = (dst if ref is None else ref, recv)

    def arrived(self, *keys):
        for key in keys:
            ref, sem = self.coming.pop(key)
            pltpu.make_async_copy(ref, ref, sem).wait()

    def fetch(self, key, src, dst, sem):
        self.local[key] = cp = pltpu.make_async_copy(src, dst, sem)
        cp.start()

    def have(self, *keys):
        for key in keys:
            self.local.pop(key).wait()

    def drain(self):
        self.have(*list(self.local))
        self.arrived(*list(self.coming))
        for ref, sem in self.sent:
            pltpu.make_async_copy(ref, ref, sem).wait()


    def ar_begin(self, r, i, top, low):
        cs = getattr(r, f"c{i}")
        cs[self.c, 0:1, :] = top
        cs[self.c, 1:2, :] = low
        mine = cs.at[self.c]
        self.put(mine, mine, r.ar_send.at[i, 0], r.ar_recv.at[i, 0], self.core_nbr, ("c", i))

    def ar_middle(self, r, i):
        cs, sl = getattr(r, f"c{i}"), getattr(r, f"s{i}")
        self.arrived(("c", i))
        sl[self.chip] = cs[0] + cs[1]
        mine = sl.at[self.chip]
        most = sl.at[pl.ds(0, self.chips - 1)]
        send, recv = r.ar_send.at[i, 1], r.ar_recv.at[i, 1]

        def one(device):
            pltpu.make_async_remote_copy(
                mine, mine, send, recv, device_id=device, device_id_type=MESH
            ).start()

        self.each_chip(one)
        self.sent.append((most, send))
        self.coming["s", i] = (most, recv)

    def ar_end(self, r, i):
        sl = getattr(r, f"s{i}")
        self.arrived(("s", i))
        if self.chips <= 16:
            total = sl[0]
            for k in range(1, self.chips):
                total = total + sl[k]
        else:
            total = lax.fori_loop(1, self.chips, lambda k, t: t + sl[k], sl[0])
        return total[0:1, :], total[1:2, :]

    def group(self, ref, flip_y=False, flip_x=False):
        y = 1 - self.y if flip_y else self.y
        x = 1 - self.x if flip_x else self.x
        return ref.at[y, x, self.c]

    def ag_pack(self, r):
        rest, tail = r.cshard[2][32:96], r.pshard[80:96, :]
        narrow = jnp.concatenate([rest[:, 32 * i : 32 * i + 32] for i in range(3)], axis=0)
        for j in range(2):
            v = jnp.concatenate([r.cshard[j], narrow[96 * j : 96 * j + 96]], axis=1)
            for h in range(2):
                g = (r.w0, r.w1, r.w2, r.w3)[2 * j + h]
                g[self.y, self.x, self.c, 0] = v[48 * h : 48 * h + 48]
        r.w4[self.y, self.x, self.c, 0, :, 0:96] = r.cshard[2][0:32]
        g5 = r.w5.at[self.y, self.x, self.c, 0]
        g5[:, 0:96] = r.pshard[0:80, :]
        g5[0:48, 96:128] = jnp.concatenate([tail[:, 32 * i : 32 * i + 32] for i in range(3)], axis=0)

    def ag_start(self, r, j):
        grp = self.group(getattr(r, f"w{j}"))
        slot, some = grp.at[0], grp.at[pl.ds(1, self.nz - 1)]
        for d in range(1, self.nz):
            pltpu.make_async_remote_copy(
                slot, grp.at[self.nz - d], r.ag_send.at[j, 0], r.ag_z.at[j],
                device_id=self.z_device(d), device_id_type=MESH,
            ).start()
        self.sent.append((some, r.ag_send.at[j, 0]))
        self.coming["z", j] = (some, r.ag_z.at[j])
        self.put(slot, slot, r.ag_send.at[j, 1], r.ag_own.at[j, 0], self.y_nbr, ("yo", j))
        self.put(slot, slot, r.ag_send.at[j, 1], r.ag_own.at[j, 1], self.x_nbr, ("xo", j))

    def to_core(self, r, j, i, grp):
        self.put(grp, grp, r.ag_send.at[j, 2], r.ag_core.at[j, i], self.core_nbr, ("core", j, i))

    def ag_plane(self, r, j):
        self.arrived(("z", j))
        grp = self.group(getattr(r, f"w{j}"))
        some = grp.at[pl.ds(1, self.nz - 1)]
        self.put(some, some, r.ag_send.at[j, 1], r.ag_oth.at[j, 0], self.y_nbr, ("yr", j))
        self.put(some, some, r.ag_send.at[j, 1], r.ag_oth.at[j, 1], self.x_nbr, ("xr", j))
        self.to_core(r, j, 0, grp)

    def ag_diagonal(self, r, j):
        g = getattr(r, f"w{j}")
        by_y, by_x = self.group(g, flip_y=True), self.group(g, flip_x=True)
        h = j % 2
        first, second = (by_y, by_x) if h == 0 else (by_x, by_y)
        self.arrived(("yx"[h] + "o", j), ("yx"[h] + "r", j))
        self.put(
            first, first, r.ag_send.at[j, 1], r.ag_d.at[j], (self.x_nbr, self.y_nbr)[h], ("d", j)
        )
        self.to_core(r, j, 1, first)
        self.arrived(("xy"[h] + "o", j), ("xy"[h] + "r", j))
        self.to_core(r, j, 2, second)

    def ag_last(self, r, j):
        self.arrived(("d", j))
        self.to_core(r, j, 3, self.group(getattr(r, f"w{j}"), True, True))

    def each_slot(self):
        for z in range(self.nz):
            at = lax.rem(z - self.z + self.nz, self.nz)
            for y in range(2):
                yield z, y, at

    def ag_unpack(self, r, k):
        H, cw, hw = self.H, self.cw, self.hw
        for j in ((0, 1), (2, 3), (4,), (5,))[k]:
            self.arrived(*[("core", j, i) for i in range(4)])
        for z, y, at in self.each_slot():
            low = (z * 2 + y) * cw
            slot = lambda j, s: r.__dict__[f"w{j}"].at[y, s // 2, s % 2, at]
            if k < 2:
                for h in range(2):
                    r.wf[low + 48 * h : low + 48 * h + 48, k * H : k * H + H] = jnp.concatenate(
                        [slot(2 * k + h, s)[:, 0:96] for s in range(4)], axis=1
                    )
            elif k == 2:
                r.wf[low : low + 32, 2 * H : 3 * H] = jnp.concatenate(
                    [slot(4, s)[:, 0:96] for s in range(4)], axis=1
                )
                for i, pieces in enumerate(
                    (((0, 0, 48), (1, 0, 16)), ((1, 16, 48), (2, 0, 32)), ((2, 32, 48), (3, 0, 48)))
                ):
                    row = low + 32
                    for j, a, b in pieces:
                        for s in range(4):
                            lane = 2 * H + s * hw + 32 * i
                            r.wf[row : row + b - a, lane : lane + 32] = slot(j, s)[a:b, 96:128]
                        row += b - a
            else:
                for s in range(4):
                    p = slot(5, s)
                    r.pf[s * hw : s * hw + 80, low : low + cw] = p[:, 0:96]
                    for i in range(3):
                        r.pf[s * hw + 80 : s * hw + 96, low + 32 * i : low + 32 * i + 32] = p[
                            16 * i : 16 * i + 16, 96:128
                        ]

    def rs_pack(self, r, cg, m):
        H, cw, hw = self.H, self.cw, self.hw
        mine = self.c == 0
        for zl in range(2):
            for y in range(2):
                low = (zl * 2 + y) * cw
                tile = lambda t, s: cg[low : low + cw, t * H + s * hw : t * H + s * hw + hw]
                for x in range(2):
                    both = []
                    for c in range(2):
                        s = x * 2 + c
                        t2 = tile(2, s)
                        rest = jnp.concatenate([t2[32:96, 32 * i : 32 * i + 32] for i in range(3)], axis=0)
                        both.append((
                            jnp.concatenate([tile(0, s), rest[0:96]], axis=1),
                            jnp.concatenate([tile(1, s), rest[96:192]], axis=1),
                            jnp.concatenate([t2[0:32], jnp.zeros((32, 32), F32)], axis=1),
                        ))
                    for a, b, at in ((both[0], both[1], 0),):
                        own = [jnp.where(mine, p, q) for p, q in zip(a, b)]
                        other = [jnp.where(mine, q, p).astype(BF) for p, q in zip(a, b)]
                    r.ra[m, 0, y, x, zl, 0:96, :] = own[0]
                    r.ra[m, 0, y, x, zl, 96:112, :] = own[1][0:16]
                    r.ra[m, 1, y, x, zl, 0:80, :] = own[1][16:96]
                    r.ra[m, 1, y, x, zl, 80:112, :] = own[2]
                    r.rs[m, 0, y, x, zl, 0:96, :] = other[0]
                    r.rs[m, 0, y, x, zl, 96:112, :] = other[1][0:16]
                    r.rs[m, 1, y, x, zl, 0:80, :] = other[1][16:96]
                    r.rs[m, 1, y, x, zl, 80:112, :] = other[2]

    def rs_core(self, r, m):
        for h in range(2):
            self.put(r.rs.at[m, h], r.rc.at[m, h], r.rs_send.at[m, h, 0], r.rs_core.at[m, h], self.core_nbr, ("rc", m, h))

    def rs_diagonal(self, r, m, h):
        self.arrived(("rc", m, h))
        for y in range(2):
            for x in range(2):
                for zl in range(2):
                    r.ra[m, h, y, x, zl] += r.rc[m, h, y, x, zl].astype(F32)
        y, x = 1 - self.y, 1 - self.x
        r.st[m, h, y, x] = r.ra[m, h, y, x].astype(BF)
        self.put(
            r.st.at[m, h, y, x], r.rd.at[m, h], r.rs_send.at[m, h, 1], r.rs_d.at[m, h],
            (self.x_nbr, self.y_nbr)[h], ("rd", m, h),
        )

    def rs_plane(self, r, m, h):
        self.arrived(("rd", m, h))
        via_y, via_x = (1 - self.y, self.x), (self.y, 1 - self.x)
        y, x = (via_y, via_x)[h]
        r.ra[m, h, y, x] += r.rd[m, h].astype(F32)
        for i, ((y, x), to) in enumerate(((via_y, self.y_nbr), (via_x, self.x_nbr))):
            r.st[m, h, y, x] = r.ra[m, h, y, x].astype(BF)
            self.put(r.st.at[m, h, y, x], r.rxy.at[m, h, i], r.rs_send.at[m, h, 2], r.rs_xy.at[m, h, i], to, ("rp", m, h, i))

    def rs_column(self, r, h):
        y, x = self.y, self.x
        for m in range(2):
            self.arrived(("rp", m, h, 0), ("rp", m, h, 1))
            r.ra[m, h, y, x] += r.rxy[m, h, 0].astype(F32) + r.rxy[m, h, 1].astype(F32)
            r.st[m, h, y, x] = r.ra[m, h, y, x].astype(BF)
        for d in range(1, self.nz):
            to = lax.rem(self.z + d, self.nz)
            pltpu.make_async_remote_copy(
                r.st.at[to // 2, h, y, x, lax.rem(to, 2)], r.rz.at[h, self.nz - d - 1],
                r.rz_send.at[h], r.rs_z.at[h], device_id=self.z_device(d), device_id_type=MESH,
            ).start()
        self.sent.append((r.rz.at[h], r.rz_send.at[h]))
        self.coming["rz", h] = (r.rz.at[h], r.rs_z.at[h])

    def rs_end(self, r):
        v = []
        for h in range(2):
            self.arrived(("rz", h))
            t = r.ra[self.z // 2, h, self.y, self.x, lax.rem(self.z, 2)]
            for i in range(3):
                t = t + r.rz[h, i].astype(F32)
            v.append(t)
        v = jnp.concatenate(v, axis=0)
        r.conv_grad[0] = v[0:96, 0:96]
        r.conv_grad[1] = v[96:192, 0:96]
        r.conv_grad[2, 0:32, :] = v[192:224, 0:96]
        for i in range(3):
            r.conv_grad[2, 32:96, 32 * i : 32 * i + 32] = v[64 * i : 64 * i + 64, 96:128]

    def pg_pack(self, r, pg):
        cw, hw = self.cw, self.hw
        mine = self.c == 0
        for z in range(self.nz):
            for y in range(2):
                lane = (z * 2 + y) * cw
                for x in range(2):
                    both = []
                    for c in range(2):
                        t = pg[(x * 2 + c) * hw : (x * 2 + c) * hw + hw, lane : lane + cw]
                        rest = jnp.concatenate([t[80:96, 32 * i : 32 * i + 32] for i in range(3)] + [jnp.zeros((32, 32), F32)], axis=0)
                        both.append(jnp.concatenate([t[0:80], rest], axis=1))
                    r.pa[y, x, z] = jnp.where(mine, both[0], both[1])
                    r.ps[y, x, z] = jnp.where(mine, both[1], both[0]).astype(BF)

    def pg_core(self, r):
        self.put(r.ps, r.pc, r.p_send.at[0], r.p_recv.at[0], self.core_nbr, "pc")

    def pg_diagonal(self, r):
        self.arrived("pc")
        for y in range(2):
            for x in range(2):
                r.pa[y, x] += r.pc[y, x].astype(F32)
        y, x = 1 - self.y, 1 - self.x
        r.pt[y, x] = r.pa[y, x].astype(BF)
        self.put(r.pt.at[y, x], r.pd, r.p_send.at[1], r.p_recv.at[1], self.x_nbr, "pd")

    def pg_plane(self, r):
        self.arrived("pd")
        via_y, via_x = (1 - self.y, self.x), (self.y, 1 - self.x)
        r.pa[via_y[0], via_y[1]] += r.pd[...].astype(F32)
        for i, ((y, x), to) in enumerate(((via_y, self.y_nbr), (via_x, self.x_nbr))):
            r.pt[y, x] = r.pa[y, x].astype(BF)
            self.put(r.pt.at[y, x], r.pxy.at[i], r.p_send.at[2], r.p_recv.at[2 + i], to, ("pp", i))

    def pg_column(self, r):
        y, x = self.y, self.x
        self.arrived(("pp", 0), ("pp", 1))
        r.pa[y, x] += r.pxy[0].astype(F32) + r.pxy[1].astype(F32)
        r.pt[y, x] = r.pa[y, x].astype(BF)
        for d in range(1, self.nz):
            to = lax.rem(self.z + d, self.nz)
            pltpu.make_async_remote_copy(
                r.pt.at[y, x, to], r.pz.at[self.nz - d - 1], r.p_send.at[3], r.p_recv.at[4],
                device_id=self.z_device(d), device_id_type=MESH,
            ).start()
        self.sent.append((r.pz, r.p_send.at[3]))
        self.coming["pz"] = (r.pz, r.p_recv.at[4])

    def pg_end(self, r):
        self.arrived("pz")
        v = r.pa[self.y, self.x, self.z]
        for i in range(3):
            v = v + r.pz[i].astype(F32)
        r.point_grad[0:80, :] = v[:, 0:96]
        for i in range(3):
            r.point_grad[80:96, 32 * i : 32 * i + 32] = v[16 * i : 16 * i + 16, 96:128]

    def halo_begin(self, r):
        R, H = self.rows, self.H
        r.hs[0] = r.big[PAD : 2 * PAD, 2 * H : 3 * H] * wide(r.mb[0:PAD], H)
        r.hs[1] = r.big[R : R + PAD, 0:H] * wide(r.ma[R - PAD : R], H)
        for j, to in enumerate((self.prev, self.next)):
            self.put(r.hs.at[j], r.halo.at[j], r.halo_send.at[0, j], r.halo_recv.at[0, j], to, ("h", j))

    def halo_end(self, r):
        R, H = self.rows, self.H
        self.arrived(("h", 0), ("h", 1))
        r.big[R + PAD : R + 2 * PAD, 2 * H : 3 * H] = r.halo[0]
        r.big[0:PAD, 0:H] = r.halo[1]

    def edges_begin(self, r):
        R, H = self.rows, self.H
        for j, (at, m, to) in enumerate(((0, r.mb, self.prev), (R - PAD, r.ma, self.next))):
            mask = m[at : at + PAD]
            r.es[j, :, 0:H] = r.p2g[at : at + PAD, :] * wide(mask, H)
            r.es[j, :, H : 2 * H] = r.conv[at : at + PAD, :] * wide(mask, H)
            r.es[j, :, 2 * H :] = mask
            self.put(r.es.at[j], r.edge.at[j], r.halo_send.at[1, j], r.halo_recv.at[1, j], to, ("e", j))

    def edges_end(self, r, a2, lin2, off2):
        R, H = self.rows, self.H
        self.arrived(("e", 0), ("e", 1))
        for j, at in ((0, R + PAD), (1, 0)):
            r.big[at : at + PAD, 0:H] = (
                r.edge[j, :, 0:H] * a2 + r.edge[j, :, H : 2 * H] * lin2 + wide(r.edge[j, :, 2 * H :], H) * off2
            )


class Refs:
    pass


def kernel(k, n_in, n_out, names, *refs):
    r = Refs()
    for name, ref in zip(names, refs[n_in + n_out :]):
        setattr(r, name, ref)
    k.sent, k.coming, k.local = [], {}, {}
    k.place()
    work(k, r, refs[:n_in], refs[n_in : n_in + n_out])
    k.drain()


def work(k, r, ins, outs):
    (x_hbm, og_hbm, species, first, sw, conv_w, point_w, g1, b1, g2, b2, run1, run2) = ins
    (out, ig, r.conv_grad, r.point_grad, gg1, gb1, gg2, gb2, new1, new2) = outs
    R, C, H, N = k.rows, k.C, k.H, k.total
    Q = R // 4
    r.bg = ig
    k.greet()
    if k.packed:
        k.fetch("cw", conv_w, r.cshard, r.insem.at[5])
        k.fetch("pw", point_w, r.pshard, r.insem.at[6])
    for q in range(4):
        rows = pl.ds(q * Q, Q)
        k.fetch(("x", q), x_hbm.at[rows], r.x.at[rows], r.insem.at[q])
    small = dict(first=first, g1=g1, b1=b1, g2=g2, b2=b2, sw=sw, run1=run1, run2=run2, species=species)
    for i, (name, ref) in enumerate(small.items()):
        k.fetch(name, ref, getattr(r, name), r.insem.at[7 + i])
    k.fetch("og", og_hbm, r.og, r.insem.at[4])
    if not k.packed:
        k.fetch("cw", conv_w, r.wf, r.insem.at[5])
        k.fetch("pw", point_w, r.pf, r.insem.at[6])
    else:
        k.have("cw", "pw")
        k.ag_pack(r)

    def sums(q):
        k.have(("x", q))
        v = r.x[q * Q : q * Q + Q, :].astype(F32)
        r.acc1[0] += colsum(v)
        r.acc1[1] += colsum(v * v)

    r.acc1[...] = jnp.zeros_like(r.acc1)
    for q in range(2):
        sums(q)
    k.greeted()
    if k.packed:
        for j in range(5):
            k.ag_start(r, j)
    for q in range(2, 4):
        sums(q)
    k.ar_begin(r, 0, squash(r.acc1[0]), squash(r.acc1[1]))

    k.have("first")
    fs = r.first[0]
    starts = [fs + SEQ_LEN * j for j in range(R // SEQ_LEN)]
    k.ar_middle(r, 0)
    if k.packed:
        k.ag_start(r, 5)

    def masks(at):
        row = row_tile(at, 128)
        before = jnp.ones((128, 128), F32)
        after = jnp.ones((128, 128), F32)
        for s in starts:
            before = jnp.where((row >= s) & (row < s + DIL), 0.0, before)
            after = jnp.where((row >= s - DIL) & (row < s), 0.0, after)
        r.mb[pl.ds(at, 128), :] = before
        r.ma[pl.ds(at, 128), :] = after

    loop(0, R, 128, masks)
    if k.packed:
        for j in range(5):
            k.ag_plane(r, j)
    k.have("g1", "b1")
    sum1, sq1 = k.ar_end(r, 0)
    mean1 = sum1 / N
    var1 = sq1 / N - mean1 * mean1
    inv1 = lax.rsqrt(var1 + EPSILON)
    gain1 = r.g1[...].reshape(1, C)
    scale1 = (HALF_SLOPE * gain1) * inv1
    shift1 = HALF_SLOPE * r.b1[...].reshape(1, C) - mean1 * scale1

    def act_tile(at):
        rows = pl.ds(at, 256)
        a, s = gelu_all(r.x[rows, :].astype(F32) * scale1 + shift1)
        r.act[rows, :] = a.astype(BF)
        r.slope[rows, :] = s.astype(BF)

    steps = (
        lambda: (k.ag_diagonal(r, 0), k.ag_diagonal(r, 1)),
        lambda: (k.ag_diagonal(r, 2), k.ag_plane(r, 5)),
        lambda: (k.ag_diagonal(r, 3), k.ag_diagonal(r, 4)),
        lambda: (k.ag_last(r, 0), k.ag_last(r, 1)),
    )
    for q in range(4):
        loop(q * Q, q * Q + Q, 256, act_tile)
        if k.packed:
            steps[q]()
    if k.packed:
        k.ag_last(r, 2)
        k.ag_unpack(r, 0)
        k.ag_last(r, 3)
        k.ag_last(r, 4)
        k.ag_unpack(r, 1)
    else:
        k.have("cw", "pw")

    def product(at, rows, lanes):
        r.big[PAD + at : PAD + at + rows, lanes] = jnp.dot(
            r.act[at : at + rows, :], r.wf[:, lanes], preferred_element_type=F32
        )

    product(0, R // 2, slice(0, 2 * H))
    if k.packed:
        k.ag_diagonal(r, 5)
    product(R // 2, R // 2, slice(0, 2 * H))
    if k.packed:
        k.ag_unpack(r, 2)
    product(0, R // 2, slice(2 * H, 3 * H))
    product(R // 2, R // 2, slice(2 * H, 3 * H))
    k.halo_begin(r)
    if k.packed:
        k.ag_last(r, 5)
    r.acc2[...] = jnp.zeros_like(r.acc2)
    T = 256

    def gather_taps(at):
        rows = pl.ds(at, T)
        lo = r.big[pl.ds(at, T + 2 * PAD), 0:H][PAD - DIL : PAD - DIL + T]
        mid = r.big[pl.ds(at + PAD, T), H : 2 * H]
        hi = r.big[pl.ds(at, T + 2 * PAD), 2 * H : 3 * H][PAD + DIL : PAD + DIL + T]
        v = lo * wide(r.mb[rows, :], H) + mid + hi * wide(r.ma[rows, :], H)
        r.conv[rows, :] = v
        r.acc2[0] += colsum(v)
        r.acc2[1] += colsum(v * v)

    loop(T, R - T, T, gather_taps)
    k.halo_end(r)
    gather_taps(0)
    gather_taps(R - T)
    k.ar_begin(r, 1, squash(r.acc2[0]), squash(r.acc2[1]))
    k.ar_middle(r, 1)

    k.have("og", "sw", "species", "g2", "b2", "run1", "run2")
    at_start = [r.species[0]] + [r.species[s] for s in starts]
    weights = [jnp.where(sp == 0, r.sw[0:1, :], r.sw[1:2, :]) for sp in at_start]

    def row_weight(at, tile):
        row = row_tile(at, tile)
        w = jnp.broadcast_to(weights[0], (tile, C))
        for s, v in zip(starts, weights[1:]):
            w = jnp.where(wide(row, C) >= s, v, w)
        return w

    def branch_grad(at):
        rows = pl.ds(at, 128)
        r.bg[rows, :] = (r.og[rows, :].astype(F32) * row_weight(at, 128)).astype(BF)

    loop(0, R, 128, branch_grad)
    if k.packed:
        k.ag_unpack(r, 3)

    def act_two_grad(at):
        rows = pl.ds(at, 1024)
        r.p2g[rows, :] = lax.dot_general(
            r.bg[rows, :], r.pf[...], (((1,), (1,)), ((), ())), preferred_element_type=F32
        )

    loop(0, R, 1024, act_two_grad)
    sum2, sq2 = k.ar_end(r, 1)
    mean2 = sum2 / N
    var2 = sq2 / N - mean2 * mean2
    inv2 = lax.rsqrt(var2 + EPSILON)
    minv2 = mean2 * inv2
    gain2 = r.g2[...].reshape(1, H)
    gain2h, bias2h = HALF_SLOPE * gain2, HALF_SLOPE * r.b2[...].reshape(1, H)
    r.acc2[...] = jnp.zeros_like(r.acc2)

    def second_norm(at):
        rows = pl.ds(at, 256)
        zh = r.conv[rows, :] * inv2 - minv2
        a, s = gelu_all(zh * gain2h + bias2h)
        r.act2[rows, :] = a.astype(BF)
        p = r.p2g[rows, :] * s
        r.p2g[rows, :] = p
        r.acc2[0] += colsum(p)
        r.acc2[1] += colsum(p * zh)

    loop(0, R, 256, second_norm)
    k.ar_begin(r, 2, squash(r.acc2[0]), squash(r.acc2[1]))
    k.edges_begin(r)
    k.ar_middle(r, 2)

    for q in range(2):
        rows = pl.ds(q * 1024, 1024)
        br = jnp.dot(r.act2[rows, :], r.pf[...], preferred_element_type=F32)
        out[rows, :] = (r.x[rows, :].astype(F32) + br).astype(BF)
    pg = lax.dot_general(
        r.act2[...], r.bg[...], (((0,), (0,)), ((), ())), preferred_element_type=F32
    )
    if k.packed:
        k.pg_pack(r, pg)
        k.pg_core(r)
    else:
        r.point_grad[...] = pg
    bsum, gsum = k.ar_end(r, 2)
    gb2[...] = bsum.reshape(H)
    gg2[...] = gsum.reshape(H)
    a2 = inv2 * gain2
    lin2 = -a2 * (gsum / N) * inv2
    off2 = -a2 * (bsum / N) + a2 * (gsum / N) * minv2

    def cot(at):
        rows = pl.ds(at, 256)
        r.big[pl.ds(at + PAD, 256), 0:H] = (
            r.p2g[rows, :] * a2 + r.conv[rows, :] * lin2 + off2
        )

    loop(0, R, 256, cot)
    if k.packed:
        k.pg_diagonal(r)
    k.edges_end(r, a2, lin2, off2)
    T2 = 128

    def shifted(at):
        rows = pl.ds(at, T2)
        v = r.big[pl.ds(at, T2 + 2 * PAD), 0:H]
        r.back[rows, 0:H] = (v[PAD + DIL : PAD + DIL + T2] * wide(r.ma[rows, :], H)).astype(BF)
        r.back[rows, H : 2 * H] = v[PAD : PAD + T2].astype(BF)
        r.back[rows, 2 * H : 3 * H] = (v[PAD - DIL : PAD - DIL + T2] * wide(r.mb[rows, :], H)).astype(BF)

    loop(0, R, T2, shifted)

    M = C // 2
    for i, m in enumerate(range(0, C, M)):
        cg = lax.dot_general(
            r.act[:, m : m + M], r.back[...], (((0,), (0,)), ((), ())), preferred_element_type=F32
        )
        if k.packed:
            k.rs_pack(r, cg, i)
            k.rs_core(r, i)
            if i == 0:
                k.pg_plane(r)
        else:
            for j in range(3):
                r.conv_grad[j, m : m + M, :] = cg[:, j * H : j * H + H]

    minv1 = mean1 * inv1
    r.acc1[...] = jnp.zeros_like(r.acc1)
    steps = (
        lambda: (k.rs_diagonal(r, 0, 0), k.rs_diagonal(r, 0, 1)),
        lambda: (k.rs_diagonal(r, 1, 0), k.rs_diagonal(r, 1, 1), k.pg_column(r)),
        lambda: (k.rs_plane(r, 0, 0), k.rs_plane(r, 0, 1)),
        lambda: None,
    )
    for q in range(4):
        rows = slice(q * Q, q * Q + Q)
        ag = lax.dot_general(
            r.back[rows, :], r.wf[...], (((1,), (1,)), ((), ())), preferred_element_type=F32
        )
        p = ag * r.slope[rows, :].astype(F32)
        r.big[rows, 0:C] = p
        r.acc1[0] += colsum(p)
        r.acc1[1] += colsum(p * (r.x[rows, :].astype(F32) * inv1 - minv1))
        if k.packed:
            steps[q]()
    k.ar_begin(r, 3, squash(r.acc1[0]), squash(r.acc1[1]))
    k.ar_middle(r, 3)
    if k.packed:
        k.rs_plane(r, 1, 0)
        k.rs_plane(r, 1, 1)
    unbias = N / (N - 1.0)
    new1[0:1, :] = MOMENTUM * r.run1[0:1, :] + (1.0 - MOMENTUM) * mean1
    new1[1:2, :] = MOMENTUM * r.run1[1:2, :] + (1.0 - MOMENTUM) * (var1 * unbias)
    new2[0:1, :] = MOMENTUM * r.run2[0:1, :] + (1.0 - MOMENTUM) * mean2
    new2[1:2, :] = MOMENTUM * r.run2[1:2, :] + (1.0 - MOMENTUM) * (var2 * unbias)
    if k.packed:
        k.pg_end(r)
    bsum1, gsum1 = k.ar_end(r, 3)
    gb1[...] = bsum1.reshape(C)
    gg1[...] = gsum1.reshape(C)
    a1 = inv1 * gain1
    lin1 = -a1 * (gsum1 / N) * inv1
    off1 = -a1 * (bsum1 / N) + a1 * (gsum1 / N) * minv1

    def last(at):
        rows = pl.ds(at, 128)
        v = r.og[rows, :].astype(F32) * row_weight(at, 128)
        v = v + r.big[rows, 0:C] * a1 + r.x[rows, :].astype(F32) * lin1 + off1
        ig[rows, :] = v.astype(BF)

    loop(0, R // 2, 128, last)
    if k.packed:
        k.rs_column(r, 0)
    if k.packed:
        k.rs_column(r, 1)
    loop(R // 2, R, 128, last)
    if k.packed:
        k.rs_end(r)


def hand_out(n, large, *refs):
    ins, outs, sems = refs[:n], refs[n : 2 * n], refs[2 * n]
    copies = [pltpu.make_async_copy(ins[i], outs[i], sems.at[i]) for i in range(n)]
    for cp in copies:
        cp.start()
    for cp in copies:
        cp.wait()


def body(
    mesh,
    activations,
    out_grad,
    species,
    first_start,
    species_weight,
    conv_weight,
    point_weight,
    gain_one,
    bias_one,
    gain_two,
    bias_two,
    running_one,
    running_two,
):
    rows, C = activations.shape
    ndp, nsub = mesh.shape["dp"], mesh.shape["sub"]
    cw, hw = conv_weight.shape[1:]
    taps, H = conv_weight.shape[0], hw * nsub
    packed = cw == 96 and hw == 96 and nsub == 4 and ndp % 2 == 0
    if not packed:
        conv_weight = lax.all_gather(conv_weight, "dp", axis=1, tiled=True)
        conv_weight = lax.all_gather(conv_weight, "sub", axis=2, tiled=True)
        conv_weight = jnp.transpose(conv_weight, (1, 0, 2)).reshape(C, taps * H)
        point_weight = lax.all_gather(point_weight, "dp", axis=1, tiled=True)
        point_weight = lax.all_gather(point_weight, "sub", axis=0, tiled=True)
    k = Kernel(mesh, rows, C, H, packed)
    scratch = k.scratch()
    here = pl.BlockSpec(memory_space=pl.ANY)
    vmem = pl.BlockSpec(memory_space=pltpu.VMEM)
    shapes = [
        ((rows, C), BF),
        ((rows, C), BF),
        ((taps, cw, hw) if packed else (taps, C, H), F32),
        ((hw, cw) if packed else (H, C), F32),
        ((C,), F32),
        ((C,), F32),
        ((H,), F32),
        ((H,), F32),
        ((2, C), F32),
        ((2, H), F32),
    ]
    held = [packed or i not in (2, 3) for i in range(len(shapes))]
    outs = pl.pallas_call(
        functools.partial(kernel, k, 13, len(shapes), list(scratch)),
        out_shape=[
            pltpu.VMEM(*s) if in_vmem else jax.ShapeDtypeStruct(*s) for s, in_vmem in zip(shapes, held)
        ],
        in_specs=[here] * 13,
        out_specs=[vmem] * len(shapes),
        scratch_shapes=list(scratch.values()),
        compiler_params=pltpu.CompilerParams(
            collective_id=0, has_side_effects=True, vmem_limit_bytes=(55 if packed else 54) * 2**20
        ),
    )(
        activations,
        out_grad,
        species,
        first_start,
        species_weight,
        conv_weight,
        point_weight,
        gain_one,
        bias_one,
        gain_two,
        bias_two,
        running_one,
        running_two,
    )
    keep = [i for i in range(len(shapes)) if held[i]]
    n = len(keep)
    given = pl.pallas_call(
        functools.partial(hand_out, n, 2),
        out_shape=[jax.ShapeDtypeStruct(*shapes[i]) for i in keep],
        in_specs=[vmem] * n,
        out_specs=[here] * n,
        scratch_shapes=[pltpu.SemaphoreType.DMA((n,))],
        compiler_params=pltpu.CompilerParams(vmem_limit_bytes=2**20),
    )(*[pltpu.with_memory_space_constraint(outs[i], pltpu.VMEM) for i in keep])
    outs = list(outs)
    for i, v in zip(keep, given):
        outs[i] = v
    if not packed:
        conv_grad, point_grad = outs[2], outs[3]
        conv_grad = lax.psum_scatter(conv_grad, "dp", scatter_dimension=1, tiled=True)
        point_grad = lax.psum_scatter(point_grad, "dp", scatter_dimension=1, tiled=True)
        outs[2] = lax.psum_scatter(conv_grad, "sub", scatter_dimension=2, tiled=True)
        outs[3] = lax.psum_scatter(point_grad, "sub", scatter_dimension=0, tiled=True)
    return tuple(outs)


def solution(mesh):
    in_specs = (
        P(("dp", "sub"), None),
        P(("dp", "sub"), None),
        P(("dp", "sub")),
        P(("dp", "sub")),
        P(),
        P(None, "dp", "sub"),
        P("sub", "dp"),
        P(),
        P(),
        P(),
        P(),
        P(),
        P(),
    )
    out_specs = (
        P(("dp", "sub"), None),
        P(("dp", "sub"), None),
        P(None, "dp", "sub"),
        P("sub", "dp"),
        P(),
        P(),
        P(),
        P(),
        P(),
        P(),
    )
    return jax.shard_map(
        functools.partial(body, mesh), mesh=mesh, in_specs=in_specs, out_specs=out_specs, check_vma=False
    )
```

time: 104 us -> 80.8 us (0.78)
  local copies, waits for them, and re-layouts: 13.1 us -> 0 us
  other arithmetic: 5.07 us -> 0 us
  Pallas kernels: 83.9 us -> 79.2 us
    unnamed x16 -> x0, local copies, waits for them, and re-layouts: 8.04 us -> none
    pallas_call x4 -> x0, other arithmetic: 5.07 us -> none  [body(): pl.pallas_call(functools.partial(kernel, k, 13, 10, list(scratch)), out_s...]
    reshape x4 -> x0, local copies, waits for them, and re-layouts: 5.02 us -> none  [body(): row = lambda v: v.reshape(1, -1)]
    pallas_call x1 -> x2, Pallas kernels: 83.9 us -> 79.2 us  [the longest x1 76.4 us: body(): pl.pallas_call(functools.partial(kernel, k, 13, len(shapes), list(scratch...]
where the time goes in v2:
time: 80.8 us; the launch traced here: 80.7 us
  Pallas kernels  79.2 us (98%)
  between operations  1.46 us (2%)
    pallas_call x1, Pallas kernels, body(): pl.pallas_call(functools.partial(kernel, k, 13, len(shapes), list(scratch...  76.4 us
    pallas_call x1, Pallas kernels, body(): pl.pallas_call(functools.partial(hand_out, n, 2), out_shape=[jax.ShapeDty...  2.84 us

profile of v2, /device:TPU:0, one launch (start us, length us, event | category | flops | bytes accessed | tf_op | source)
XLA Modules:
  0.0 80.7 jit_solution(14246815283779264797)
XLA Ops:
  1.3 76.4 %shard_map.204 = (bf16[2048,768]{1,0:T(8,128)(2,1)S(1)}, bf16[2048,768]{1,0:T(8,128)(2,1)S(1)}, f32[3,96,96]{2,1,0:T(8,128)S(1)}, f32[96,96]{1,0:T(8,128)S(1)}, ...) custom-call(bf16[2048,768]{1,0:T(8,128)(2,1)} %refs_0_.1, ...), custom_call_target="tpu_custom_call" | custom-call | tf_op jit(solution)/shard_map/pallas_call | solution.py:893
  77.7 2.8 %shard_map.205 = (bf16[2048,768]{1,0:T(8,128)(2,1)}, bf16[2048,768]{1,0:T(8,128)(2,1)}, f32[3,96,96]{2,1,0:T(8,128)}, f32[96,96]{1,0:T(8,128)}, f32[768]{0:T(102...) custom-call(bf16[2048,768]{1,0:T(8,128)(2,1)S(1)} %get-tuple-element.20.refs_0_, ...), custom_call_target="tpu_custom_call" | custom-call | tf_op jit(solution)/shard_map/pallas_call | solution.py:921

commit v3 on v2

--- a/solution.py
+++ b/solution.py
@@ -49,6 +49,41 @@
 
 def wide(m, n):
     return jnp.concatenate([m] * (n // 128), axis=1)
+
+
+def lanes_of(rows):
+    return lax.broadcasted_iota(jnp.int32, (rows, 128), 1)
+
+
+def join(pieces):
+    lane = lanes_of(pieces[0].shape[0])
+    return [jnp.where(lane < 96 - 32 * i, pieces[i], pieces[i + 1]) for i in range(3)]
+
+
+def split(tiles):
+    lane = lanes_of(tiles[0].shape[0])
+    return [
+        tiles[0],
+        jnp.where(lane >= 96, tiles[0], tiles[1]),
+        jnp.where(lane >= 64, tiles[1], tiles[2]),
+        tiles[2],
+    ]
+
+
+def free(i, lane):
+    at = (96 * i + 96) % 128
+    return (lane >= at) & (lane < at + 32)
+
+
+def narrow(v, i):
+    return pltpu.roll(v, 96 - 32 * i, 1)
+
+
+def widen(blocks, i):
+    lane = lanes_of(blocks[0].shape[0])
+    moved = [pltpu.roll(b, 32 + 32 * j, 1) for j, b in enumerate(blocks)]
+    inside = lambda j: (lane >= (96 * i + 32 * j) % 128) & (lane < (96 * i + 32 * j) % 128 + 32)
+    return jnp.where(inside(0), moved[0], jnp.where(inside(1), moved[1], moved[2]))
 
 
 class Kernel:
@@ -265,17 +300,19 @@
         return ref.at[y, x, self.c]
 
     def ag_pack(self, r):
-        rest, tail = r.cshard[2][32:96], r.pshard[80:96, :]
-        narrow = jnp.concatenate([rest[:, 32 * i : 32 * i + 32] for i in range(3)], axis=0)
+        lane = lanes_of(96)
+        full = lambda v: jnp.concatenate([v.astype(F32), jnp.zeros((96, 32), F32)], axis=1)
+        place = lambda v, i: pltpu.roll(v, lax.rem(96 * i, 128), 1).astype(BF)
+        here = (self.y, self.x, self.c, 0)
+        t2, p = full(r.cshard[2]), full(r.pshard[...])
+        rest = jnp.concatenate([narrow(t2, i)[32:96] for i in range(3)], axis=0)
         for j in range(2):
-            v = jnp.concatenate([r.cshard[j], narrow[96 * j : 96 * j + 96]], axis=1)
+            v = place(jnp.where(lane < 96, full(r.cshard[j]), rest[96 * j : 96 * j + 96]), self.sub)
             for h in range(2):
-                g = (r.w0, r.w1, r.w2, r.w3)[2 * j + h]
-                g[self.y, self.x, self.c, 0] = v[48 * h : 48 * h + 48]
-        r.w4[self.y, self.x, self.c, 0, :, 0:96] = r.cshard[2][0:32]
-        g5 = r.w5.at[self.y, self.x, self.c, 0]
-        g5[:, 0:96] = r.pshard[0:80, :]
-        g5[0:48, 96:128] = jnp.concatenate([tail[:, 32 * i : 32 * i + 32] for i in range(3)], axis=0)
+                (r.w0, r.w1, r.w2, r.w3)[2 * j + h][here] = v[48 * h : 48 * h + 48]
+        r.w4[here] = place(t2[0:32], self.sub)
+        rest = jnp.concatenate([narrow(p[80:96], i) for i in range(3)] + [jnp.zeros((32, 128), F32)], axis=0)
+        r.w5[here] = place(jnp.where(lane[0:80] < 96, p[0:80], rest), self.dp)
 
     def ag_start(self, r, j):
         grp = self.group(getattr(r, f"w{j}"))
@@ -328,65 +365,71 @@
         H, cw, hw = self.H, self.cw, self.hw
         for j in ((0, 1), (2, 3), (4,), (5,))[k]:
             self.arrived(*[("core", j, i) for i in range(4)])
-        for z, y, at in self.each_slot():
-            low = (z * 2 + y) * cw
-            slot = lambda j, s: r.__dict__[f"w{j}"].at[y, s // 2, s % 2, at]
-            if k < 2:
-                for h in range(2):
-                    r.wf[low + 48 * h : low + 48 * h + 48, k * H : k * H + H] = jnp.concatenate(
-                        [slot(2 * k + h, s)[:, 0:96] for s in range(4)], axis=1
-                    )
-            elif k == 2:
-                r.wf[low : low + 32, 2 * H : 3 * H] = jnp.concatenate(
-                    [slot(4, s)[:, 0:96] for s in range(4)], axis=1
-                )
-                for i, pieces in enumerate(
-                    (((0, 0, 48), (1, 0, 16)), ((1, 16, 48), (2, 0, 32)), ((2, 32, 48), (3, 0, 48)))
-                ):
-                    row = low + 32
-                    for j, a, b in pieces:
-                        for s in range(4):
-                            lane = 2 * H + s * hw + 32 * i
-                            r.wf[row : row + b - a, lane : lane + 32] = slot(j, s)[a:b, 96:128]
-                        row += b - a
-            else:
-                for s in range(4):
-                    p = slot(5, s)
-                    r.pf[s * hw : s * hw + 80, low : low + cw] = p[:, 0:96]
-                    for i in range(3):
-                        r.pf[s * hw + 80 : s * hw + 96, low + 32 * i : low + 32 * i + 32] = p[
-                            16 * i : 16 * i + 16, 96:128
-                        ]
+
+        def slot(j, y, s, at):
+            return getattr(r, f"w{j}").at[y, s // 2, s % 2, at]
+
+        def keep(ref, row, lane, tiles):
+            for i, t in enumerate(tiles):
+                ref[row : row + t.shape[0], lane + 128 * i : lane + 128 * i + 128] = t.astype(BF)
+
+        if k < 3:
+            for z, y, at in self.each_slot():
+                low = (z * 2 + y) * cw
+                if k < 2:
+                    for h in range(2):
+                        tiles = join([slot(2 * k + h, y, s, at)[...].astype(F32) for s in range(4)])
+                        keep(r.wf, low + 48 * h, k * H, tiles)
+                else:
+                    keep(r.wf, low, 2 * H, join([slot(4, y, s, at)[...].astype(F32) for s in range(4)]))
+                    pieces = []
+                    for s in range(4):
+                        parts = [slot(j, y, s, at) for j in range(4)]
+                        cut = lambda j, a, b: parts[j][a:b, :].astype(F32)
+                        pieces.append(widen((
+                            jnp.concatenate([cut(0, 0, 48), cut(1, 0, 16)], axis=0),
+                            jnp.concatenate([cut(1, 16, 48), cut(2, 0, 32)], axis=0),
+                            jnp.concatenate([cut(2, 32, 48), cut(3, 0, 48)], axis=0),
+                        ), s))
+                    keep(r.wf, low + 32, 2 * H, join(pieces))
+        else:
+            ats = {z: at for z, _, at in self.each_slot()}
+            for s in range(4):
+                for q in range(2):
+                    got = [slot(5, dp % 2, s, ats[dp // 2])[...].astype(F32) for dp in range(4 * q, 4 * q + 4)]
+                    keep(r.pf, s * hw, 4 * q * cw, join([v[0:80] for v in got]))
+                    rest = [widen([v[16 * i : 16 * i + 16] for i in range(3)], dp) for dp, v in enumerate(got)]
+                    keep(r.pf, s * hw + 80, 4 * q * cw, join(rest))
 
     def rs_pack(self, r, cg, m):
-        H, cw, hw = self.H, self.cw, self.hw
+        H, cw = self.H, self.cw
         mine = self.c == 0
+        lane = lanes_of(96)
         for zl in range(2):
             for y in range(2):
                 low = (zl * 2 + y) * cw
-                tile = lambda t, s: cg[low : low + cw, t * H + s * hw : t * H + s * hw + hw]
+                taps = [
+                    split([cg[low : low + cw, t * H + 128 * i : t * H + 128 * i + 128] for i in range(3)])
+                    for t in range(3)
+                ]
                 for x in range(2):
                     both = []
-                    for c in range(2):
-                        s = x * 2 + c
-                        t2 = tile(2, s)
-                        rest = jnp.concatenate([t2[32:96, 32 * i : 32 * i + 32] for i in range(3)], axis=0)
+                    for s in (2 * x, 2 * x + 1):
+                        t2 = taps[2][s]
+                        rest = jnp.concatenate([narrow(t2[32:96], i) for i in range(3)], axis=0)
+                        gap = free(s, lane)
                         both.append((
-                            jnp.concatenate([tile(0, s), rest[0:96]], axis=1),
-                            jnp.concatenate([tile(1, s), rest[96:192]], axis=1),
-                            jnp.concatenate([t2[0:32], jnp.zeros((32, 32), F32)], axis=1),
+                            jnp.where(gap, rest[0:96], taps[0][s]),
+                            jnp.where(gap, rest[96:192], taps[1][s]),
+                            t2[0:32],
                         ))
-                    for a, b, at in ((both[0], both[1], 0),):
-                        own = [jnp.where(mine, p, q) for p, q in zip(a, b)]
-                        other = [jnp.where(mine, q, p).astype(BF) for p, q in zip(a, b)]
-                    r.ra[m, 0, y, x, zl, 0:96, :] = own[0]
-                    r.ra[m, 0, y, x, zl, 96:112, :] = own[1][0:16]
-                    r.ra[m, 1, y, x, zl, 0:80, :] = own[1][16:96]
-                    r.ra[m, 1, y, x, zl, 80:112, :] = own[2]
-                    r.rs[m, 0, y, x, zl, 0:96, :] = other[0]
-                    r.rs[m, 0, y, x, zl, 96:112, :] = other[1][0:16]
-                    r.rs[m, 1, y, x, zl, 0:80, :] = other[1][16:96]
-                    r.rs[m, 1, y, x, zl, 80:112, :] = other[2]
+                    own = [jnp.where(mine, p, q) for p, q in zip(*both)]
+                    other = [jnp.where(mine, q, p).astype(BF) for p, q in zip(*both)]
+                    for ref, v in ((r.ra, own), (r.rs, other)):
+                        ref[m, 0, y, x, zl, 0:96, :] = v[0]
+                        ref[m, 0, y, x, zl, 96:112, :] = v[1][0:16]
+                        ref[m, 1, y, x, zl, 0:80, :] = v[1][16:96]
+                        ref[m, 1, y, x, zl, 80:112, :] = v[2]
 
     def rs_core(self, r, m):
         for h in range(2):
@@ -414,20 +457,25 @@
             r.st[m, h, y, x] = r.ra[m, h, y, x].astype(BF)
             self.put(r.st.at[m, h, y, x], r.rxy.at[m, h, i], r.rs_send.at[m, h, 2], r.rs_xy.at[m, h, i], to, ("rp", m, h, i))
 
-    def rs_column(self, r, h):
+    def rs_column(self, r, m, h):
         y, x = self.y, self.x
-        for m in range(2):
-            self.arrived(("rp", m, h, 0), ("rp", m, h, 1))
-            r.ra[m, h, y, x] += r.rxy[m, h, 0].astype(F32) + r.rxy[m, h, 1].astype(F32)
-            r.st[m, h, y, x] = r.ra[m, h, y, x].astype(BF)
-        for d in range(1, self.nz):
-            to = lax.rem(self.z + d, self.nz)
-            pltpu.make_async_remote_copy(
-                r.st.at[to // 2, h, y, x, lax.rem(to, 2)], r.rz.at[h, self.nz - d - 1],
-                r.rz_send.at[h], r.rs_z.at[h], device_id=self.z_device(d), device_id_type=MESH,
-            ).start()
-        self.sent.append((r.rz.at[h], r.rz_send.at[h]))
-        self.coming["rz", h] = (r.rz.at[h], r.rs_z.at[h])
+        self.arrived(("rp", m, h, 0), ("rp", m, h, 1))
+        r.ra[m, h, y, x] += r.rxy[m, h, 0].astype(F32) + r.rxy[m, h, 1].astype(F32)
+        r.st[m, h, y, x] = r.ra[m, h, y, x].astype(BF)
+        for zl in range(2):
+            to = 2 * m + zl
+            d = lax.rem(self.z - to + self.nz, self.nz)
+
+            @pl.when(d != 0)
+            def _():
+                pltpu.make_async_remote_copy(
+                    r.st.at[m, h, y, x, zl], r.rz.at[h, d - 1], r.rz_send.at[h], r.rs_z.at[h],
+                    device_id=(to * 2 + self.y, self.sub), device_id_type=MESH,
+                ).start()
+
+        if m == 1:
+            self.sent.append((r.rz.at[h], r.rz_send.at[h]))
+            self.coming["rz", h] = (r.rz.at[h], r.rs_z.at[h])
 
     def rs_end(self, r):
         v = []
@@ -437,27 +485,33 @@
             for i in range(3):
                 t = t + r.rz[h, i].astype(F32)
             v.append(t)
-        v = jnp.concatenate(v, axis=0)
+        v = pltpu.roll(jnp.concatenate(v, axis=0), lax.rem(128 - lax.rem(96 * self.sub, 128), 128), 1)
         r.conv_grad[0] = v[0:96, 0:96]
         r.conv_grad[1] = v[96:192, 0:96]
         r.conv_grad[2, 0:32, :] = v[192:224, 0:96]
-        for i in range(3):
-            r.conv_grad[2, 32:96, 32 * i : 32 * i + 32] = v[64 * i : 64 * i + 64, 96:128]
+        r.conv_grad[2, 32:96, :] = widen([v[64 * i : 64 * i + 64] for i in range(3)], 0)[:, 0:96]
 
     def pg_pack(self, r, pg):
         cw, hw = self.cw, self.hw
         mine = self.c == 0
-        for z in range(self.nz):
-            for y in range(2):
-                lane = (z * 2 + y) * cw
-                for x in range(2):
-                    both = []
-                    for c in range(2):
-                        t = pg[(x * 2 + c) * hw : (x * 2 + c) * hw + hw, lane : lane + cw]
-                        rest = jnp.concatenate([t[80:96, 32 * i : 32 * i + 32] for i in range(3)] + [jnp.zeros((32, 32), F32)], axis=0)
-                        both.append(jnp.concatenate([t[0:80], rest], axis=1))
-                    r.pa[y, x, z] = jnp.where(mine, both[0], both[1])
-                    r.ps[y, x, z] = jnp.where(mine, both[1], both[0]).astype(BF)
+        lane = lanes_of(80)
+        pieces = []
+        for s in range(4):
+            rows = slice(s * hw, s * hw + hw)
+            pieces.append([
+                p
+                for q in range(2)
+                for p in split([pg[rows, 4 * q * cw + 128 * i : 4 * q * cw + 128 * i + 128] for i in range(3)])
+            ])
+        for dp in range(self.ndp):
+            for x in range(2):
+                both = []
+                for s in (2 * x, 2 * x + 1):
+                    p = pieces[s][dp]
+                    rest = jnp.concatenate([narrow(p[80:96], i) for i in range(3)] + [p[0:32]], axis=0)
+                    both.append(jnp.where(free(dp, lane), rest, p[0:80]))
+                r.pa[dp % 2, x, dp // 2] = jnp.where(mine, both[0], both[1])
+                r.ps[dp % 2, x, dp // 2] = jnp.where(mine, both[1], both[0]).astype(BF)
 
     def pg_core(self, r):
         self.put(r.ps, r.pc, r.p_send.at[0], r.p_recv.at[0], self.core_nbr, "pc")
@@ -498,16 +552,19 @@
         v = r.pa[self.y, self.x, self.z]
         for i in range(3):
             v = v + r.pz[i].astype(F32)
+        v = pltpu.roll(v, lax.rem(128 - lax.rem(96 * self.dp, 128), 128), 1)
         r.point_grad[0:80, :] = v[:, 0:96]
-        for i in range(3):
-            r.point_grad[80:96, 32 * i : 32 * i + 32] = v[16 * i : 16 * i + 16, 96:128]
-
-    def halo_begin(self, r):
+        r.point_grad[80:96, :] = widen([v[16 * i : 16 * i + 16] for i in range(3)], 0)[:, 0:96]
+
+    def halo_up(self, r):
         R, H = self.rows, self.H
+        r.hs[1] = r.big[R : R + PAD, 0:H] * wide(r.ma[R - PAD : R], H)
+        self.put(r.hs.at[1], r.halo.at[1], r.halo_send.at[0, 1], r.halo_recv.at[0, 1], self.next, ("h", 1))
+
+    def halo_down(self, r):
+        H = self.H
         r.hs[0] = r.big[PAD : 2 * PAD, 2 * H : 3 * H] * wide(r.mb[0:PAD], H)
-        r.hs[1] = r.big[R : R + PAD, 0:H] * wide(r.ma[R - PAD : R], H)
-        for j, to in enumerate((self.prev, self.next)):
-            self.put(r.hs.at[j], r.halo.at[j], r.halo_send.at[0, j], r.halo_recv.at[0, j], to, ("h", j))
+        self.put(r.hs.at[0], r.halo.at[0], r.halo_send.at[0, 0], r.halo_recv.at[0, 0], self.prev, ("h", 0))
 
     def halo_end(self, r):
         R, H = self.rows, self.H
@@ -592,9 +649,6 @@
     fs = r.first[0]
     starts = [fs + SEQ_LEN * j for j in range(R // SEQ_LEN)]
     k.ar_middle(r, 0)
-    if k.packed:
-        k.ag_start(r, 5)
-
     def masks(at):
         row = row_tile(at, 128)
         before = jnp.ones((128, 128), F32)
@@ -609,6 +663,7 @@
     if k.packed:
         for j in range(5):
             k.ag_plane(r, j)
+        k.ag_start(r, 5)
     k.have("g1", "b1")
     sum1, sq1 = k.ar_end(r, 0)
     mean1 = sum1 / N
@@ -620,14 +675,15 @@
 
     def act_tile(at):
         rows = pl.ds(at, 256)
-        a, s = gelu_all(r.x[rows, :].astype(F32) * scale1 + shift1)
+        u = r.x[rows, :].astype(F32) * scale1 + shift1
+        a, s = gelu_all(u)
         r.act[rows, :] = a.astype(BF)
         r.slope[rows, :] = s.astype(BF)
 
     steps = (
         lambda: (k.ag_diagonal(r, 0), k.ag_diagonal(r, 1)),
-        lambda: (k.ag_diagonal(r, 2), k.ag_plane(r, 5)),
-        lambda: (k.ag_diagonal(r, 3), k.ag_diagonal(r, 4)),
+        lambda: (k.ag_diagonal(r, 2), k.ag_diagonal(r, 3)),
+        lambda: (k.ag_diagonal(r, 4), k.ag_plane(r, 5)),
         lambda: (k.ag_last(r, 0), k.ag_last(r, 1)),
     )
     for q in range(4):
@@ -636,8 +692,8 @@
             steps[q]()
     if k.packed:
         k.ag_last(r, 2)
+        k.ag_last(r, 3)
         k.ag_unpack(r, 0)
-        k.ag_last(r, 3)
         k.ag_last(r, 4)
         k.ag_unpack(r, 1)
     else:
@@ -649,16 +705,15 @@
         )
 
     product(0, R // 2, slice(0, 2 * H))
+    product(R // 2, R // 2, slice(0, 2 * H))
+    if k.packed:
+        k.ag_unpack(r, 2)
+    k.halo_up(r)
+    product(0, R // 2, slice(2 * H, 3 * H))
+    k.halo_down(r)
+    product(R // 2, R // 2, slice(2 * H, 3 * H))
     if k.packed:
         k.ag_diagonal(r, 5)
-    product(R // 2, R // 2, slice(0, 2 * H))
-    if k.packed:
-        k.ag_unpack(r, 2)
-    product(0, R // 2, slice(2 * H, 3 * H))
-    product(R // 2, R // 2, slice(2 * H, 3 * H))
-    k.halo_begin(r)
-    if k.packed:
-        k.ag_last(r, 5)
     r.acc2[...] = jnp.zeros_like(r.acc2)
     T = 256
 
@@ -678,6 +733,8 @@
     gather_taps(R - T)
     k.ar_begin(r, 1, squash(r.acc2[0]), squash(r.acc2[1]))
     k.ar_middle(r, 1)
+    if k.packed:
+        k.ag_last(r, 5)
 
     k.have("og", "sw", "species", "g2", "b2", "run1", "run2")
     at_start = [r.species[0]] + [r.species[s] for s in starts]
@@ -729,10 +786,12 @@
     k.edges_begin(r)
     k.ar_middle(r, 2)
 
-    for q in range(2):
-        rows = pl.ds(q * 1024, 1024)
-        br = jnp.dot(r.act2[rows, :], r.pf[...], preferred_element_type=F32)
-        out[rows, :] = (r.x[rows, :].astype(F32) + br).astype(BF)
+    def block_output():
+        for q in range(2):
+            rows = pl.ds(q * 1024, 1024)
+            br = jnp.dot(r.act2[rows, :], r.pf[...], preferred_element_type=F32)
+            out[rows, :] = (r.x[rows, :].astype(F32) + br).astype(BF)
+
     pg = lax.dot_general(
         r.act2[...], r.bg[...], (((0,), (0,)), ((), ())), preferred_element_type=F32
     )
@@ -785,12 +844,15 @@
 
     minv1 = mean1 * inv1
     r.acc1[...] = jnp.zeros_like(r.acc1)
+    both = lambda f, m: (f(r, m, 0), f(r, m, 1))
     steps = (
-        lambda: (k.rs_diagonal(r, 0, 0), k.rs_diagonal(r, 0, 1)),
-        lambda: (k.rs_diagonal(r, 1, 0), k.rs_diagonal(r, 1, 1), k.pg_column(r)),
-        lambda: (k.rs_plane(r, 0, 0), k.rs_plane(r, 0, 1)),
+        lambda: both(k.rs_diagonal, 1),
+        lambda: k.pg_column(r),
+        lambda: both(k.rs_plane, 0),
         lambda: None,
     )
+    if k.packed:
+        both(k.rs_diagonal, 0)
     for q in range(4):
         rows = slice(q * Q, q * Q + Q)
         ag = lax.dot_general(
@@ -805,15 +867,15 @@
     k.ar_begin(r, 3, squash(r.acc1[0]), squash(r.acc1[1]))
     k.ar_middle(r, 3)
     if k.packed:
-        k.rs_plane(r, 1, 0)
-        k.rs_plane(r, 1, 1)
+        both(k.rs_plane, 1)
+    block_output()
+    if k.packed:
+        both(k.rs_column, 0)
     unbias = N / (N - 1.0)
     new1[0:1, :] = MOMENTUM * r.run1[0:1, :] + (1.0 - MOMENTUM) * mean1
     new1[1:2, :] = MOMENTUM * r.run1[1:2, :] + (1.0 - MOMENTUM) * (var1 * unbias)
     new2[0:1, :] = MOMENTUM * r.run2[0:1, :] + (1.0 - MOMENTUM) * mean2
     new2[1:2, :] = MOMENTUM * r.run2[1:2, :] + (1.0 - MOMENTUM) * (var2 * unbias)
-    if k.packed:
-        k.pg_end(r)
     bsum1, gsum1 = k.ar_end(r, 3)
     gb1[...] = bsum1.reshape(C)
     gg1[...] = gsum1.reshape(C)
@@ -827,13 +889,12 @@
         v = v + r.big[rows, 0:C] * a1 + r.x[rows, :].astype(F32) * lin1 + off1
         ig[rows, :] = v.astype(BF)
 
+    if k.packed:
+        both(k.rs_column, 1)
     loop(0, R // 2, 128, last)
-    if k.packed:
-        k.rs_column(r, 0)
-    if k.packed:
-        k.rs_column(r, 1)
     loop(R // 2, R, 128, last)
     if k.packed:
+        k.pg_end(r)
         k.rs_end(r)
 
 

time: 80.8 us -> 73.5 us (0.910)
  Pallas kernels: 79.2 us -> 71.9 us
    pallas_call x1, Pallas kernels: 76.4 us -> 69.1 us  [body(): pl.pallas_call(functools.partial(kernel, k, 13, len(shapes), list(scratch...]
where the time goes in v3:
time: 73.5 us; the launch traced here: 73.4 us
  Pallas kernels  71.9 us (98%)
  between operations  1.46 us (2%)
    pallas_call x1, Pallas kernels, body(): pl.pallas_call(functools.partial(kernel, k, 13, len(shapes), list(scratch...  69.1 us
    pallas_call x1, Pallas kernels, body(): pl.pallas_call(functools.partial(hand_out, n, 2), out_shape=[jax.ShapeDty...  2.84 us

profile of v3, /device:TPU:0, one launch (start us, length us, event | category | flops | bytes accessed | tf_op | source)
XLA Modules:
  0.0 73.4 jit_solution(11329246644842365926)
XLA Ops:
  1.3 69.1 %shard_map.204 = (bf16[2048,768]{1,0:T(8,128)(2,1)S(1)}, bf16[2048,768]{1,0:T(8,128)(2,1)S(1)}, f32[3,96,96]{2,1,0:T(8,128)S(1)}, f32[96,96]{1,0:T(8,128)S(1)}, ...) custom-call(bf16[2048,768]{1,0:T(8,128)(2,1)} %refs_0_.1, ...), custom_call_target="tpu_custom_call" | custom-call | tf_op jit(solution)/shard_map/pallas_call | solution.py:954
  70.4 2.8 %shard_map.205 = (bf16[2048,768]{1,0:T(8,128)(2,1)}, bf16[2048,768]{1,0:T(8,128)(2,1)}, f32[3,96,96]{2,1,0:T(8,128)}, f32[96,96]{1,0:T(8,128)}, f32[768]{0:T(102...) custom-call(bf16[2048,768]{1,0:T(8,128)(2,1)S(1)} %get-tuple-element.20.refs_0_, ...), custom_call_target="tpu_custom_call" | custom-call | tf_op jit(solution)/shard_map/pallas_call | solution.py:982

commit v4 on v3

--- a/solution.py
+++ b/solution.py
@@ -155,17 +155,17 @@
                 ag_oth=D((len(PARTS), 2)),
                 ag_d=D((len(PARTS),)),
                 ag_core=D((len(PARTS), 4)),
-                ra=V((2, 2, 2, 2, 2, SIDE, 128), F32),
-                rs=V((2, 2, 2, 2, 2, SIDE, 128), BF),
-                rc=V((2, 2, 2, 2, 2, SIDE, 128), BF),
-                st=V((2, 2, 2, 2, 2, SIDE, 128), BF),
-                rd=V((2, 2, 2, SIDE, 128), BF),
-                rxy=V((2, 2, 2, 2, SIDE, 128), BF),
+                ra=V((nz, 2, 2, 2, SIDE, 128), F32),
+                rs=V((nz, 2, 2, 2, SIDE, 128), BF),
+                rc=V((nz, 2, 2, 2, SIDE, 128), BF),
+                st=V((nz, 2, 2, 2, SIDE, 128), BF),
+                rd=V((nz, 2, SIDE, 128), BF),
+                rxy=V((nz, 2, 2, SIDE, 128), BF),
                 rz=V((2, 3, SIDE, 128), BF),
-                rs_send=D((2, 2, 3)),
-                rs_core=D((2, 2)),
-                rs_d=D((2, 2)),
-                rs_xy=D((2, 2, 2)),
+                rs_send=D((nz, 2, 3)),
+                rs_core=D((nz, 2)),
+                rs_d=D((nz, 2)),
+                rs_xy=D((nz, 2, 2)),
                 rz_send=D((2,)),
                 rs_z=D((2,)),
                 pa=V((2, 2, nz, 80, 128), F32),
@@ -401,35 +401,34 @@
                     rest = [widen([v[16 * i : 16 * i + 16] for i in range(3)], dp) for dp, v in enumerate(got)]
                     keep(r.pf, s * hw + 80, 4 * q * cw, join(rest))
 
-    def rs_pack(self, r, cg, m):
+    def rs_pack(self, r, cg, m, first):
         H, cw = self.H, self.cw
         mine = self.c == 0
         lane = lanes_of(96)
-        for zl in range(2):
-            for y in range(2):
-                low = (zl * 2 + y) * cw
-                taps = [
-                    split([cg[low : low + cw, t * H + 128 * i : t * H + 128 * i + 128] for i in range(3)])
-                    for t in range(3)
-                ]
-                for x in range(2):
-                    both = []
-                    for s in (2 * x, 2 * x + 1):
-                        t2 = taps[2][s]
-                        rest = jnp.concatenate([narrow(t2[32:96], i) for i in range(3)], axis=0)
-                        gap = free(s, lane)
-                        both.append((
-                            jnp.where(gap, rest[0:96], taps[0][s]),
-                            jnp.where(gap, rest[96:192], taps[1][s]),
-                            t2[0:32],
-                        ))
-                    own = [jnp.where(mine, p, q) for p, q in zip(*both)]
-                    other = [jnp.where(mine, q, p).astype(BF) for p, q in zip(*both)]
-                    for ref, v in ((r.ra, own), (r.rs, other)):
-                        ref[m, 0, y, x, zl, 0:96, :] = v[0]
-                        ref[m, 0, y, x, zl, 96:112, :] = v[1][0:16]
-                        ref[m, 1, y, x, zl, 0:80, :] = v[1][16:96]
-                        ref[m, 1, y, x, zl, 80:112, :] = v[2]
+        for y in range(2):
+            low = first + y * cw
+            taps = [
+                split([cg[low : low + cw, t * H + 128 * i : t * H + 128 * i + 128] for i in range(3)])
+                for t in range(3)
+            ]
+            for x in range(2):
+                both = []
+                for s in (2 * x, 2 * x + 1):
+                    t2 = taps[2][s]
+                    rest = jnp.concatenate([narrow(t2[32:96], i) for i in range(3)], axis=0)
+                    gap = free(s, lane)
+                    both.append((
+                        jnp.where(gap, rest[0:96], taps[0][s]),
+                        jnp.where(gap, rest[96:192], taps[1][s]),
+                        t2[0:32],
+                    ))
+                own = [jnp.where(mine, p, q) for p, q in zip(*both)]
+                other = [jnp.where(mine, q, p).astype(BF) for p, q in zip(*both)]
+                for ref, v in ((r.ra, own), (r.rs, other)):
+                    ref[m, 0, y, x, 0:96, :] = v[0]
+                    ref[m, 0, y, x, 96:112, :] = v[1][0:16]
+                    ref[m, 1, y, x, 0:80, :] = v[1][16:96]
+                    ref[m, 1, y, x, 80:112, :] = v[2]
 
     def rs_core(self, r, m):
         for h in range(2):
@@ -439,8 +438,7 @@
         self.arrived(("rc", m, h))
         for y in range(2):
             for x in range(2):
-                for zl in range(2):
-                    r.ra[m, h, y, x, zl] += r.rc[m, h, y, x, zl].astype(F32)
+                r.ra[m, h, y, x] += r.rc[m, h, y, x].astype(F32)
         y, x = 1 - self.y, 1 - self.x
         r.st[m, h, y, x] = r.ra[m, h, y, x].astype(BF)
         self.put(
@@ -462,18 +460,16 @@
         self.arrived(("rp", m, h, 0), ("rp", m, h, 1))
         r.ra[m, h, y, x] += r.rxy[m, h, 0].astype(F32) + r.rxy[m, h, 1].astype(F32)
         r.st[m, h, y, x] = r.ra[m, h, y, x].astype(BF)
-        for zl in range(2):
-            to = 2 * m + zl
-            d = lax.rem(self.z - to + self.nz, self.nz)
-
-            @pl.when(d != 0)
-            def _():
-                pltpu.make_async_remote_copy(
-                    r.st.at[m, h, y, x, zl], r.rz.at[h, d - 1], r.rz_send.at[h], r.rs_z.at[h],
-                    device_id=(to * 2 + self.y, self.sub), device_id_type=MESH,
-                ).start()
-
-        if m == 1:
+        d = lax.rem(self.z - m + self.nz, self.nz)
+
+        @pl.when(d != 0)
+        def _():
+            pltpu.make_async_remote_copy(
+                r.st.at[m, h, y, x], r.rz.at[h, d - 1], r.rz_send.at[h], r.rs_z.at[h],
+                device_id=(m * 2 + self.y, self.sub), device_id_type=MESH,
+            ).start()
+
+        if m == self.nz - 1:
             self.sent.append((r.rz.at[h], r.rz_send.at[h]))
             self.coming["rz", h] = (r.rz.at[h], r.rs_z.at[h])
 
@@ -481,7 +477,7 @@
         v = []
         for h in range(2):
             self.arrived(("rz", h))
-            t = r.ra[self.z // 2, h, self.y, self.x, lax.rem(self.z, 2)]
+            t = r.ra[self.z, h, self.y, self.x]
             for i in range(3):
                 t = t + r.rz[h, i].astype(F32)
             v.append(t)
@@ -834,8 +830,9 @@
             r.act[:, m : m + M], r.back[...], (((0,), (0,)), ((), ())), preferred_element_type=F32
         )
         if k.packed:
-            k.rs_pack(r, cg, i)
-            k.rs_core(r, i)
+            for z in range(2):
+                k.rs_pack(r, cg, 2 * i + z, z * (M // 2))
+                k.rs_core(r, 2 * i + z)
             if i == 0:
                 k.pg_plane(r)
         else:
@@ -844,15 +841,15 @@
 
     minv1 = mean1 * inv1
     r.acc1[...] = jnp.zeros_like(r.acc1)
-    both = lambda f, m: (f(r, m, 0), f(r, m, 1))
+    both = lambda f, *ms: [f(r, m, h) for m in ms for h in range(2)]
     steps = (
-        lambda: both(k.rs_diagonal, 1),
-        lambda: k.pg_column(r),
+        lambda: both(k.rs_diagonal, 2, 3),
         lambda: both(k.rs_plane, 0),
-        lambda: None,
+        lambda: (both(k.rs_plane, 1, 2), k.pg_column(r)),
+        lambda: both(k.rs_plane, 3),
     )
     if k.packed:
-        both(k.rs_diagonal, 0)
+        both(k.rs_diagonal, 0, 1)
     for q in range(4):
         rows = slice(q * Q, q * Q + Q)
         ag = lax.dot_general(
@@ -867,10 +864,10 @@
     k.ar_begin(r, 3, squash(r.acc1[0]), squash(r.acc1[1]))
     k.ar_middle(r, 3)
     if k.packed:
-        both(k.rs_plane, 1)
+        both(k.rs_column, 0, 1)
     block_output()
     if k.packed:
-        both(k.rs_column, 0)
+        both(k.rs_column, 2)
     unbias = N / (N - 1.0)
     new1[0:1, :] = MOMENTUM * r.run1[0:1, :] + (1.0 - MOMENTUM) * mean1
     new1[1:2, :] = MOMENTUM * r.run1[1:2, :] + (1.0 - MOMENTUM) * (var1 * unbias)
@@ -890,9 +887,8 @@
         ig[rows, :] = v.astype(BF)
 
     if k.packed:
-        both(k.rs_column, 1)
-    loop(0, R // 2, 128, last)
-    loop(R // 2, R, 128, last)
+        both(k.rs_column, 3)
+    loop(0, R, 128, last)
     if k.packed:
         k.pg_end(r)
         k.rs_end(r)

time: 73.5 us -> 73.1 us (level)
  no operation moved by 1% of the time
where the time goes in v4:
time: 73.1 us; the launch traced here: 73 us
  Pallas kernels  71.5 us (98%)
  between operations  1.46 us (2%)
    pallas_call x1, Pallas kernels, body(): pl.pallas_call(functools.partial(kernel, k, 13, len(shapes), list(scratch...  68.7 us
    pallas_call x1, Pallas kernels, body(): pl.pallas_call(functools.partial(hand_out, n, 2), out_shape=[jax.ShapeDty...  2.84 us

profile of v4, /device:TPU:0, one launch (start us, length us, event | category | flops | bytes accessed | tf_op | source)
XLA Modules:
  0.0 73.0 jit_solution(3026261119840285111)
XLA Ops:
  1.3 68.7 %shard_map.204 = (bf16[2048,768]{1,0:T(8,128)(2,1)S(1)}, bf16[2048,768]{1,0:T(8,128)(2,1)S(1)}, f32[3,96,96]{2,1,0:T(8,128)S(1)}, f32[96,96]{1,0:T(8,128)S(1)}, ...) custom-call(bf16[2048,768]{1,0:T(8,128)(2,1)} %refs_0_.1, ...), custom_call_target="tpu_custom_call" | custom-call | tf_op jit(solution)/shard_map/pallas_call | solution.py:950
  70.0 2.8 %shard_map.205 = (bf16[2048,768]{1,0:T(8,128)(2,1)}, bf16[2048,768]{1,0:T(8,128)(2,1)}, f32[3,96,96]{2,1,0:T(8,128)}, f32[96,96]{1,0:T(8,128)}, f32[768]{0:T(102...) custom-call(bf16[2048,768]{1,0:T(8,128)(2,1)S(1)} %get-tuple-element.20.refs_0_, ...), custom_call_target="tpu_custom_call" | custom-call | tf_op jit(solution)/shard_map/pallas_call | solution.py:978

commit v5 on v4

--- a/solution.py
+++ b/solution.py
@@ -631,13 +631,11 @@
         r.acc1[1] += colsum(v * v)
 
     r.acc1[...] = jnp.zeros_like(r.acc1)
-    for q in range(2):
-        sums(q)
     k.greeted()
     if k.packed:
         for j in range(5):
             k.ag_start(r, j)
-    for q in range(2, 4):
+    for q in range(4):
         sums(q)
     k.ar_begin(r, 0, squash(r.acc1[0]), squash(r.acc1[1]))
 

time: 73.1 us -> 73.1 us (level)
  no operation moved by 1% of the time
where the time goes in v5:
time: 73.1 us; the launch traced here: 72.9 us
  Pallas kernels  71.4 us (98%)
  between operations  1.46 us (2%)
    pallas_call x1, Pallas kernels, body(): pl.pallas_call(functools.partial(kernel, k, 13, len(shapes), list(scratch...  68.6 us
    pallas_call x1, Pallas kernels, body(): pl.pallas_call(functools.partial(hand_out, n, 2), out_shape=[jax.ShapeDty...  2.84 us

profile of v5, /device:TPU:0, one launch (start us, length us, event | category | flops | bytes accessed | tf_op | source)
XLA Modules:
  0.0 72.9 jit_solution(1929412279335691992)
XLA Ops:
  1.3 68.6 %shard_map.204 = (bf16[2048,768]{1,0:T(8,128)(2,1)S(1)}, bf16[2048,768]{1,0:T(8,128)(2,1)S(1)}, f32[3,96,96]{2,1,0:T(8,128)S(1)}, f32[96,96]{1,0:T(8,128)S(1)}, ...) custom-call(bf16[2048,768]{1,0:T(8,128)(2,1)} %refs_0_.1, ...), custom_call_target="tpu_custom_call" | custom-call | tf_op jit(solution)/shard_map/pallas_call | solution.py:948
  69.9 2.8 %shard_map.205 = (bf16[2048,768]{1,0:T(8,128)(2,1)}, bf16[2048,768]{1,0:T(8,128)(2,1)}, f32[3,96,96]{2,1,0:T(8,128)}, f32[96,96]{1,0:T(8,128)}, f32[768]{0:T(102...) custom-call(bf16[2048,768]{1,0:T(8,128)(2,1)S(1)} %get-tuple-element.20.refs_0_, ...), custom_call_target="tpu_custom_call" | custom-call | tf_op jit(solution)/shard_map/pallas_call | solution.py:976
